TPU v7x, 128 devices: a whole 4x4x4 slice. The times are simulated.
128 devices in a mesh: lat: 4 (over y_hi, core), lon: 32 (over z, y_lo, x).
Axes of the slice: x: 4, y: 4 (y_hi: 2, y_lo: 2; y = y_hi * 2 + y_lo), z: 4, core: 2. Of those that a mesh axis runs over, the one named last changes fastest.
Arguments:
- tokens: bfloat16 [4, 24, 384, 512], P(None, 'lat', 'lon'), may hold values from -9 to 9
- region_ids: int32 [24, 384], P('lat', 'lon'), may hold values from 0 to 3
- shift_lat: int32 [4], replicated, may hold values from 1 to 5
- shift_lon: int32 [4], replicated, may hold values from 1 to 11
- gain_attn: float32 [512], replicated, may hold values from 0.25 to 1.75
- w_qkv: bfloat16 [512, 1536], replicated, may hold values from -1 to 1
- w_out: bfloat16 [512, 512], replicated, may hold values from -0.25 to 0.25
- gain_mlp: float32 [512], replicated, may hold values from 0.25 to 1.75
- w_up: bfloat16 [512, 2048], replicated, may hold values from -0.25 to 0.25
- w_down: bfloat16 [2048, 512], replicated, may hold values from -0.125 to 0.125
- cotangent: bfloat16 [4, 24, 384, 512], P(None, 'lat', 'lon'), may hold values from -6 to 6
Outputs:
- block_out: bfloat16 [4, 24, 384, 512], P(None, 'lat', 'lon')
- grad_tokens: bfloat16 [4, 24, 384, 512], P(None, 'lat', 'lon')
- grad_gain_attn: float32 [512], replicated
- grad_qkv: float32 [512, 1536], replicated
- grad_out: float32 [512, 512], replicated
- grad_gain_mlp: float32 [512], replicated
- grad_up: float32 [512, 2048], replicated
- grad_down: float32 [2048, 512], replicated
Inputs may be any that keep to these rules, and one draw needn't show every extreme that they name: `region_ids`: a query attends only to keys of its window whose region number is equal to its own.
All inputs are finite; a program needn't handle non-finite values.
Results may differ from a plain program's by a relative error of at most 0.014.
The roundings to bfloat16 on the way count: a program that leaves them out, or rounds other values in their place, can miss the bound.
Values may be sent and summed in bfloat16 or wider, within the bound.
A program may use at most 192 MiB of HBM per device.

v0:
```python
import jax
import jax.numpy as jnp
from jax import lax
from jax.sharding import PartitionSpec as P

HEADS = 8
WV = 2
WH = 6
WW = 12


EPS = 1e-05
DIMS_ZERO = (((0,), (0,)), ((), ()))
DIMS_LAST = (((1,), (1,)), ((), ()))


def shifted(value, axis, by):
    devices = lax.axis_size(axis)
    return lax.ppermute(value, axis, [(i, (i + by) % devices) for i in range(devices)])


def norm_stats(values):
    center = values - jnp.mean(values, axis=-1, keepdims=True)
    inv_scale = lax.rsqrt(jnp.mean(center * center, axis=-1, keepdims=True) + EPS)
    return (center * inv_scale, inv_scale)


def norm_back(grad, normed, inv_scale, gain):
    gain_grad = jnp.sum((grad * normed).reshape(-1, grad.shape[-1]), axis=0)
    graded = grad * gain
    term = inv_scale * (
        graded
        - jnp.mean(graded, axis=-1, keepdims=True)
        - normed * jnp.mean(graded * normed, axis=-1, keepdims=True)
    )
    return (term, gain_grad)


def gelu_value(inner):
    return 0.5 * inner * (1.0 + lax.erf(inner * 0.7071067811865476))


def gelu_slope(inner):
    return (
        0.5 * (1.0 + lax.erf(inner * 0.7071067811865476))
        + inner * jnp.exp(-0.5 * inner * inner) * 0.3989422804014327
    )


def cut_levels(field, rows, cols, lat_rows, lon_cols):
    planes = []
    for level in range(field.shape[0]):
        plane = field[level]
        starts = (rows[level], cols[level]) + tuple((jnp.int32(0) for _ in plane.shape[2:]))
        planes.append(lax.dynamic_slice(plane, starts, (lat_rows, lon_cols) + plane.shape[2:]))
    return jnp.stack(planes)


def to_frame(field, labels, row_shift, col_shift):
    levels, lat_rows, lon_cols, feats = field.shape
    above, above_ids = shifted((field, labels), "lat", 1)
    field = jnp.concatenate([above, field], axis=1)
    labels = jnp.concatenate([above_ids, labels], axis=1)
    left, left_ids = shifted((field, labels), "lon", 1)
    field = jnp.concatenate([left, field], axis=2)
    labels = jnp.concatenate([left_ids, labels], axis=2)
    start_row = WH - row_shift
    start_col = WW - col_shift
    field = cut_levels(field, start_row, start_col, lat_rows, lon_cols)
    labels = cut_levels(labels, start_row, start_col, lat_rows, lon_cols)
    return (field, labels)


def to_data(field, row_shift, col_shift):
    levels, lat_rows, lon_cols, feats = field.shape
    below = shifted(field, "lat", -1)
    field = jnp.concatenate([field, below], axis=1)
    right = shifted(field, "lon", -1)
    field = jnp.concatenate([field, right], axis=2)
    return cut_levels(field, row_shift, col_shift, lat_rows, lon_cols)


def window_view(field, width):
    levels, lat_rows, lon_cols = field.shape[:3]
    head_size = width // HEADS
    return field.reshape(
        levels // WV, WV, lat_rows // WH, WH, lon_cols // WW, WW, -1, HEADS, head_size
    )


def window_mask(frame_ids):
    levels, lat_rows, lon_cols = frame_ids.shape
    grouped = frame_ids.reshape(levels // WV, WV, lat_rows // WH, WH, lon_cols // WW, WW)
    grouped = grouped.transpose(0, 2, 4, 1, 3, 5).reshape(
        levels // WV, lat_rows // WH, lon_cols // WW, WV * WH * WW
    )
    return (grouped[..., :, None] == grouped[..., None, :])[:, :, :, None]


def attend(qkv_field, allowed, width):
    view = window_view(qkv_field, width)
    query, keyset, values = (view[..., 0, :, :], view[..., 1, :, :], view[..., 2, :, :])
    factor = (width // HEADS) ** (-0.5)
    win_cells = WV * WH * WW
    scores = jnp.einsum(
        "avbhcwne,aubgcxne->abcnvhwugx", query, keyset, preferred_element_type=jnp.float32
    )
    lead = scores.shape[:4]
    scores = scores.reshape(lead + (win_cells, win_cells)) * factor
    scores = jnp.where(allowed, scores, -jnp.inf)
    peak = jnp.max(scores, axis=-1, keepdims=True)
    expo = jnp.exp(scores - peak)
    probs = expo / jnp.sum(expo, axis=-1, keepdims=True)
    weights = probs.astype(jnp.bfloat16)
    split_w = weights.reshape(lead + (WV, WH, WW, WV, WH, WW))
    mixed = jnp.einsum(
        "abcnvhwugx,aubgcxne->avbhcwne", split_w, values, preferred_element_type=jnp.float32
    )
    return (mixed.astype(jnp.bfloat16).reshape(-1, width), probs, weights, view)


def attend_back(grad_mixed, view, probs, weights, width):
    query, keyset, values = (view[..., 0, :, :], view[..., 1, :, :], view[..., 2, :, :])
    factor = (width // HEADS) ** (-0.5)
    win_cells = WV * WH * WW
    dgrad = grad_mixed.reshape(query.shape)
    lead = probs.shape[:4]
    grad_probs = jnp.einsum(
        "avbhcwne,aubgcxne->abcnvhwugx", dgrad, values, preferred_element_type=jnp.float32
    )
    grad_probs = grad_probs.reshape(lead + (win_cells, win_cells))
    split_w = weights.reshape(lead + (WV, WH, WW, WV, WH, WW))
    grad_values = jnp.einsum(
        "abcnvhwugx,avbhcwne->aubgcxne", split_w, dgrad, preferred_element_type=jnp.float32
    )
    grad_scores = (
        probs * (grad_probs - jnp.sum(grad_probs * probs, axis=-1, keepdims=True)) * factor
    ).astype(jnp.bfloat16)
    split_s = grad_scores.reshape(lead + (WV, WH, WW, WV, WH, WW))
    grad_query = jnp.einsum(
        "abcnvhwugx,aubgcxne->avbhcwne", split_s, keyset, preferred_element_type=jnp.float32
    )
    grad_keys = jnp.einsum(
        "abcnvhwugx,avbhcwne->aubgcxne", split_s, query, preferred_element_type=jnp.float32
    )
    joined = jnp.stack([grad_query, grad_keys, grad_values], axis=-3)
    return joined.astype(jnp.bfloat16).reshape(-1, 3 * width)


def on_device(
    tokens,
    region_ids,
    shift_lat,
    shift_lon,
    gain_attn,
    w_qkv,
    w_out,
    gain_mlp,
    w_up,
    w_down,
    cotangent,
):
    levels, lat_rows, lon_cols, model_width = tokens.shape
    start_state = tokens.astype(jnp.float32)
    normed_a, scale_a = norm_stats(start_state)
    h_attn = (normed_a * gain_attn).astype(jnp.bfloat16)
    id_field = jnp.broadcast_to(region_ids[None, :, :], (levels, lat_rows, lon_cols))
    frame_h, frame_ids = to_frame(h_attn, id_field, shift_lat, shift_lon)
    allowed = window_mask(frame_ids)
    flat_h = frame_h.reshape(-1, model_width)
    qkv = jnp.dot(flat_h, w_qkv, preferred_element_type=jnp.float32).astype(jnp.bfloat16)
    mixed, probs, weights, view = attend(
        qkv.reshape(levels, lat_rows, lon_cols, 3 * model_width), allowed, model_width
    )
    attn = jnp.dot(mixed, w_out, preferred_element_type=jnp.float32).astype(jnp.bfloat16)
    attn_back = to_data(attn.reshape(levels, lat_rows, lon_cols, model_width), shift_lat, shift_lon)
    resid = start_state + attn_back.astype(jnp.float32)
    normed_m, scale_m = norm_stats(resid)
    h_mlp = (normed_m * gain_mlp).astype(jnp.bfloat16)
    flat_m = h_mlp.reshape(-1, model_width)
    pre = jnp.dot(flat_m, w_up, preferred_element_type=jnp.float32)
    act = gelu_value(pre).astype(jnp.bfloat16)
    lifted = jnp.dot(act, w_down, preferred_element_type=jnp.float32)
    block_out = (resid + lifted.reshape(levels, lat_rows, lon_cols, model_width)).astype(
        jnp.bfloat16
    )
    cot_flat = cotangent.reshape(-1, model_width)
    grad_down = lax.dot_general(act, cot_flat, DIMS_ZERO, preferred_element_type=jnp.float32)
    grad_act = lax.dot_general(cot_flat, w_down, DIMS_LAST, preferred_element_type=jnp.float32)
    grad_pre = (grad_act * gelu_slope(pre)).astype(jnp.bfloat16)
    grad_up = lax.dot_general(flat_m, grad_pre, DIMS_ZERO, preferred_element_type=jnp.float32)
    dh_mlp = lax.dot_general(grad_pre, w_up, DIMS_LAST, preferred_element_type=jnp.float32)
    term_m, grad_gain_mlp = norm_back(
        dh_mlp.reshape(levels, lat_rows, lon_cols, model_width), normed_m, scale_m, gain_mlp
    )
    grad_resid = cotangent.astype(jnp.float32) + term_m
    grad_attn, _ = to_frame(grad_resid.astype(jnp.bfloat16), id_field, shift_lat, shift_lon)
    grad_attn = grad_attn.reshape(-1, model_width)
    grad_out = lax.dot_general(mixed, grad_attn, DIMS_ZERO, preferred_element_type=jnp.float32)
    grad_mixed = lax.dot_general(
        grad_attn, w_out, DIMS_LAST, preferred_element_type=jnp.float32
    ).astype(jnp.bfloat16)
    grad_cells = attend_back(grad_mixed, view, probs, weights, model_width)
    grad_qkv = lax.dot_general(flat_h, grad_cells, DIMS_ZERO, preferred_element_type=jnp.float32)
    grad_frame = lax.dot_general(
        grad_cells, w_qkv, DIMS_LAST, preferred_element_type=jnp.float32
    ).astype(jnp.bfloat16)
    grad_h = to_data(
        grad_frame.reshape(levels, lat_rows, lon_cols, model_width), shift_lat, shift_lon
    ).astype(jnp.float32)
    term_a, grad_gain_attn = norm_back(grad_h, normed_a, scale_a, gain_attn)
    grad_tokens = (grad_resid + term_a).astype(jnp.bfloat16)
    grad_qkv, grad_out, grad_gain_attn, grad_up, grad_down, grad_gain_mlp = lax.psum(
        (grad_qkv, grad_out, grad_gain_attn, grad_up, grad_down, grad_gain_mlp), ("lat", "lon")
    )
    return (
        block_out,
        grad_tokens,
        grad_gain_attn,
        grad_qkv,
        grad_out,
        grad_gain_mlp,
        grad_up,
        grad_down,
    )


def solution(mesh):
    placed = (
        P(None, "lat", "lon", None),
        P("lat", "lon"),
        P(),
        P(),
        P(),
        P(),
        P(),
        P(),
        P(),
        P(),
        P(None, "lat", "lon", None),
    )
    return jax.shard_map(
        on_device,
        mesh=mesh,
        in_specs=placed,
        out_specs=(
            P(None, "lat", "lon", None),
            P(None, "lat", "lon", None),
            P(),
            P(),
            P(),
            P(),
            P(),
            P(),
        ),
        check_vma=False,
    )
```

profile of v0, /device:TPU:1, one launch (start us, length us, event | category | flops | bytes accessed | tf_op | source)
XLA Modules:
  0.0 432.5 jit_solution(13775747091231364544)
XLA Ops:
  8.1 4.3 collective-permute-start.2
  38.4 16.5 %collective-permute-done.1 = bf16[4,12,12,512]{3,0,2,1:T(4,128)(2,1)S(1)} collective-permute-done((bf16[4,12,12,512]{3,0,2,1:T(4,128)(2,1)S(1)}, bf16[4,12,12,512]{3,0,2,1:T(4,128)(2,1)S(1)}, u32[]{:S(2)}, u32[]{:S(2)}) %collective-permute-start.1) | collective-permute-done | bytes 589856 | tf_op jit(solution)/shard_map/ppermute | solution.py:19
  55.9 3.1 convolution_convert_fusion
  59.0 3.6 reshape_reshape.3
  64.2 9.1 %fusion = (f32[2,8,2,6,12]{4,3,2,1,0:T(8,128)S(1)}, f32[2,8,2,6,12,2,6,12]{4,7,6,5,3,2,1,0:T(8,128)}) fusion(pred[2,2,6,12,2,6,12]{3,6,5,4,2,1,0:T(8,128)(4,1)S(1)} %broadcast_compare_fusion, bf16[2,2,1,6,1,12,1,8,64]{8,7,6,5,3,1,0,4,2:T(8,128)(2,1)S(1)} %get-tuple-element.44, bf16[2,2,1,6,1,12,1,8,64]{8,7,6,5,3,1,0,4,2:T(8,128)(2,1)S(1)} %get-tuple-element.45), kind=kOutput, calls=%fused_computation.4 | convolution fusion | flops 43460352 | bytes 1967616 | tf_op jit(solution)/shard_map/avbhcwne,aubgcxne->abcnvhwugx/dot_general | solution.py:105
  73.2 12.6 %fusion.2 = f32[2,8,2,6,12]{4,3,2,1,0:T(8,128)S(1)} fusion(f32[2,8,2,6,12,2,6,12]{4,7,6,5,3,2,1,0:T(8,128)} %get-tuple-element.89, f32[2,8,2,6,12]{4,3,2,1,0:T(8,128)S(1)} %get-tuple-element.88, pred[2,2,6,12,2,6,12]{3,6,5,4,2,1,0:T(8,128)(4,1)S(1)} %broadcast_compare_fusion), kind=kLoop, calls=%fused_computation.6 | loop fusion | flops 1324800 | bytes 1387008 | tf_op jit(solution)/shard_map/reduce_sum | solution.py:113
  85.8 9.4 %fusion.56 = bf16[2,8,2,6,12,2,6,12]{4,7,6,5,3,2,1,0:T(8,128)(2,1)S(1)} fusion(f32[2,8,2,6,12]{4,3,2,1,0:T(8,128)S(1)} %fusion.2, f32[2,8,2,6,12]{4,3,2,1,0:T(8,128)S(1)} %get-tuple-element.88, f32[2,8,2,6,12,2,6,12]{4,7,6,5,3,2,1,0:T(8,128)} %get-tuple-element.89, pred[2,2,6,12,2,6,12]{3,6,5,4,2,1,0:T(8,128)(4,1)S(1)} %broadcast_compare_fusion), kind=kLoop, calls=%fused_computation.142 | loop fusion | flops 1658880 | bytes 2050560 | tf_op jit(solution)/shard_map/convert_element_type | solution.py:114
  107.1 6.2 %collective-permute-done.4 = bf16[4,6,12,512]{3,2,1,0:T(8,128)(2,1)S(1)} collective-permute-done((bf16[4,6,12,512]{3,2,1,0:T(8,128)(2,1)}, bf16[4,6,12,512]{3,2,1,0:T(8,128)(2,1)S(1)}, u32[]{:S(2)}, u32[]{:S(2)}) %collective-permute-start.4) | collective-permute-done | bytes 294944 | tf_op jit(solution)/shard_map/ppermute | solution.py:19
  149.0 3.2 fusion.65
  157.4 4.7 %collective-permute-done.6 = bf16[4,6,12,512]{3,2,1,0:T(8,128)(2,1)S(1)} collective-permute-done((bf16[4,6,12,512]{3,2,1,0:T(8,128)(2,1)S(1)}, bf16[4,6,12,512]{3,2,1,0:T(8,128)(2,1)S(1)}, u32[]{:S(2)}, u32[]{:S(2)}) %collective-permute-start.6) | collective-permute-done | bytes 294944 | tf_op jit(solution)/shard_map/ppermute | solution.py:19
  163.0 3.3 fusion.68
  166.3 3.3 fusion.69
  169.6 10.5 %collective-permute-done.7 = bf16[4,12,12,512]{3,0,2,1:T(4,128)(2,1)S(1)} collective-permute-done((bf16[4,12,12,512]{3,0,2,1:T(4,128)(2,1)S(1)}, bf16[4,12,12,512]{3,0,2,1:T(4,128)(2,1)S(1)}, u32[]{:S(2)}, u32[]{:S(2)}) %collective-permute-start.7) | collective-permute-done | bytes 589856 | tf_op jit(solution)/shard_map/ppermute | solution.py:19
  183.4 6.8 %fusion.19 = bf16[2,8,64,2,6,12]{2,5,4,3,1,0:T(8,128)(2,1)S(1)} fusion(bf16[2,8,2,6,12,2,6,12]{4,7,6,5,3,2,1,0:T(8,128)(2,1)} %copy-done.2, bf16[2,2,6,12,8,64,1,1]{5,4,3,2,1,0,7,6:T(8,128)(2,1)} %bitcast.135), kind=kOutput, calls=%fused_computation.28 | convolution fusion | flops 42467328 | bytes 1253376 | tf_op jit(solution)/shard_map/abcnvhwugx,avbhcwne->aubgcxne/dot_general | solution.py:133
  190.2 17.8 %multiply_reduce_fusion = (f32[2,8,2,6,12]{4,3,2,1,0:T(8,128)S(1)}, f32[2,8,2,6,12,2,6,12]{4,7,6,5,3,2,1,0:T(8,128)}) fusion(f32[2,8,2,6,12]{4,3,2,1,0:T(8,128)S(1)} %copy-done.31, f32[2,8,2,6,12]{4,3,2,1,0:T(8,128)S(1)} %copy-done.24, f32[2,8,2,6,12,2,6,12]{4,7,6,5,3,2,1,0:T(8,128)} %get-tuple-element.89, ...), kind=kOutput, calls=%fused_computation.1 | convolution fusion | flops 44455680 | bytes 3313152 | tf_op jit(solution)/shard_map/avbhcwne,aubgcxne->abcnvhwugx/dot_general | solution.py:128
  208.0 14.5 %multiply_convert_fusion = bf16[2,8,2,6,12,2,6,12]{4,7,6,5,3,2,1,0:T(8,128)(2,1)S(1)} fusion(f32[2,8,2,6,12,2,6,12]{4,7,6,5,3,2,1,0:T(8,128)} %get-tuple-element.95, f32[2,8,2,6,12]{4,3,2,1,0:T(8,128)S(1)} %get-tuple-element.94, f32[2,8,2,6,12]{4,3,2,1,0:T(8,128)S(1)} %copy-done.31, f32[2,8,2,6,12]{4,3,2,1,0:T(8,128)S(1)} %copy-done.24, ...), kind=kLoop, calls=%fused_computation | loop fusion | flops 2654208 | bytes 3386880 | tf_op jit(solution)/shard_map/convert_element_type | solution.py:138
  222.5 2.9 fusion.16
  232.3 3.0 convert_element_type.110
  240.2 2.9 collective-permute-start.8
  243.1 8.4 %collective-permute-done.8 = bf16[4,6,12,512]{3,2,1,0:T(8,128)(2,1)S(1)} collective-permute-done((bf16[4,6,12,512]{3,2,1,0:T(8,128)(2,1)S(1)}, bf16[4,6,12,512]{3,2,1,0:T(8,128)(2,1)S(1)}, u32[]{:S(2)}, u32[]{:S(2)}) %collective-permute-start.8) | collective-permute-done | bytes 294944 | tf_op jit(solution)/shard_map/ppermute | solution.py:19
  253.1 17.7 %collective-permute-done.9 = bf16[4,12,12,512]{3,0,2,1:T(4,128)(2,1)S(1)} collective-permute-done((bf16[4,12,12,512]{3,0,2,1:T(4,128)(2,1)S(1)}, bf16[4,12,12,512]{3,0,2,1:T(4,128)(2,1)S(1)}, u32[]{:S(2)}, u32[]{:S(2)}) %collective-permute-start.9) | collective-permute-done | bytes 589856 | tf_op jit(solution)/shard_map/ppermute | solution.py:19
  274.0 67.0 %all-reduce = (f32[512]{0:T(512)}, f32[512]{0:T(512)}) all-reduce(f32[512]{0:T(512)S(1)} %get-tuple-element.34, f32[512]{0:T(512)S(1)} %copy-done.43), channel_id=1, replica_groups=mesh['lat'=4,'lon'=32] {'lat','lon'}, use_global_device_ids=true, to_apply=%region_12.13 | all-reduce | flops 1024 | bytes 8192 | tf_op jit(solution)/shard_map/psum | solution.py:213
  341.0 73.9 %all-reduce.4.cloned.1.call-done = (f32[512,1536]{1,0:T(8,128)}, f32[512,512]{1,0:T(8,128)}, f32[512,2048]{1,0:T(8,128)}, f32[2048,512]{1,0:T(8,128)}) async-done(((f32[512,1536]{1,0:T(8,128)}, f32[512,512]{1,0:T(8,128)}, f32[512,2048]{1,0:T(8,128)}, f32[2048,512]{1,0:T(8,128)}), (f32[512,1536]{1,0:T(8,128)}, f32[512,512]{1,0:T(8,128)}, f32[512,2048]{1,0:T(8,128)}, ...) | async-done | bytes 12582928 | tf_op jit(solution)/shard_map/psum | solution.py:213
  414.9 3.9 copy.232
  (211 shorter events, 78.4 us)
Async XLA Ops:
  7.2 133.5 %copy-start = (bf16[512,2048]{1,0:T(8,128)(2,1)S(1)}, bf16[512,2048]{1,0:T(8,128)(2,1)}, u32[]{:S(2)}) copy-start(bf16[512,2048]{1,0:T(8,128)(2,1)} %param.19) | copy-start | bytes 6291460
  7.2 407.7 %all-reduce.4.cloned.1.call-start = ((), (), s32[]{:S(2)}) async-start(), calls=%async_computation | async-start | bytes 25165824 | tf_op jit(solution)/shard_map/psum | solution.py:213
  8.1 10.4 %collective-permute-start.2 = (s32[4,6,12]{2,1,0:T(8,128)S(1)}, s32[4,6,12]{2,1,0:T(8,128)S(1)}, u32[]{:S(2)}, u32[]{:S(2)}) collective-permute-start(s32[4,6,12]{2,1,0:T(8,128)S(1)} %broadcast_in_dim.10), channel_id=1, source_target_pairs={{0,32},{32,64},{64,96},{96,0},{1,33},{33,65},{65,97},{97,1},{2,34}... | collective-permute-start | bytes 3464 | tf_op jit(solution)/shard_map/ppermute | solution.py:19
  16.5 19.5 %collective-permute-start = (bf16[4,6,12,512]{3,2,1,0:T(8,128)(2,1)S(1)}, bf16[4,6,12,512]{3,2,1,0:T(8,128)(2,1)S(1)}, u32[]{:S(2)}, u32[]{:S(2)}) collective-permute-start(bf16[4,6,12,512]{3,2,1,0:T(8,128)(2,1)S(1)} %fusion.38), channel_id=1, source_target_pairs={{0,32},{32,64},{64,96},{96,0},{1,33},{33,65},{65,97},{97,1},{2,34}... | collective-permute-start | bytes 884744 | tf_op jit(solution)/shard_map/ppermute | solution.py:19
  18.5 17.4 %collective-permute-start.3 = (s32[4,12,12]{2,1,0:T(8,128)S(1)}, s32[4,12,12]{2,1,0:T(8,128)S(1)}, u32[]{:S(2)}, u32[]{:S(2)}) collective-permute-start(s32[4,12,12]{2,1,0:T(8,128)S(1)} %pad_add_fusion), channel_id=1, source_target_pairs={{0,1},{1,2},{2,3},{3,4},{4,5},{5,6},{6,7},{7,8},{8,9},{9,10},{10,1... | collective-permute-start | bytes 6920 | tf_op jit(solution)/shard_map/ppermute | solution.py:19
  36.6 18.4 %collective-permute-start.1 = (bf16[4,12,12,512]{3,0,2,1:T(4,128)(2,1)S(1)}, bf16[4,12,12,512]{3,0,2,1:T(4,128)(2,1)S(1)}, u32[]{:S(2)}, u32[]{:S(2)}) collective-permute-start(bf16[4,12,12,512]{3,0,2,1:T(4,128)(2,1)S(1)} %copy.85), channel_id=1, source_target_pairs={{0,1},{1,2},{2,3},{3,4},{4,5},{5,6},{6,7},{7,8},{8,9},{9,10},{10,1... | collective-permute-start | bytes 1769480 | tf_op jit(solution)/shard_map/ppermute | solution.py:19
  64.1 9.1 %copy-start.5 = (bf16[2,2,1,6,1,12,1,8,64]{8,7,6,5,3,1,0,4,2:T(8,128)(2,1)}, bf16[2,2,1,6,1,12,1,8,64]{8,7,6,5,3,1,0,4,2:T(8,128)(2,1)S(1)}, u32[]{:S(2)}) copy-start(bf16[2,2,1,6,1,12,1,8,64]{8,7,6,5,3,1,0,4,2:T(8,128)(2,1)S(1)} %get-tuple-element.44) | copy-start | bytes 884740
  64.1 9.1 %copy-start.8 = (bf16[2,2,1,6,1,12,1,8,64]{8,7,6,5,3,1,0,4,2:T(8,128)(2,1)}, bf16[2,2,1,6,1,12,1,8,64]{8,7,6,5,3,1,0,4,2:T(8,128)(2,1)S(1)}, u32[]{:S(2)}) copy-start(bf16[2,2,1,6,1,12,1,8,64]{8,7,6,5,3,1,0,4,2:T(8,128)(2,1)S(1)} %get-tuple-element.45) | copy-start | bytes 884740
  64.2 31.1 %copy-start.16 = (bf16[2,2,1,6,1,12,1,8,64]{8,7,6,5,3,1,0,4,2:T(8,128)(2,1)}, bf16[2,2,1,6,1,12,1,8,64]{8,7,6,5,3,1,0,4,2:T(8,128)(2,1)S(1)}, u32[]{:S(2)}) copy-start(bf16[2,2,1,6,1,12,1,8,64]{8,7,6,5,3,1,0,4,2:T(8,128)(2,1)S(1)} %get-tuple-element.43) | copy-start | bytes 884740
  73.2 12.6 %copy-start.23 = (f32[2,8,2,6,12]{4,3,2,1,0:T(8,128)}, f32[2,8,2,6,12]{4,3,2,1,0:T(8,128)S(1)}, u32[]{:S(2)}) copy-start(f32[2,8,2,6,12]{4,3,2,1,0:T(8,128)S(1)} %get-tuple-element.88) | copy-start | bytes 27652
  85.8 9.4 %copy-start.30 = (f32[2,8,2,6,12]{4,3,2,1,0:T(8,128)}, f32[2,8,2,6,12]{4,3,2,1,0:T(8,128)S(1)}, u32[]{:S(2)}) copy-start(f32[2,8,2,6,12]{4,3,2,1,0:T(8,128)S(1)} %fusion.2) | copy-start | bytes 27652
  101.6 14.1 %copy-start.44 = (s32[4]{0:T(128)S(1)}, s32[4]{0:T(128)}, u32[]{:S(2)}) copy-start(s32[4]{0:T(128)} %param.13) | copy-start | bytes 52
  101.6 15.9 %copy-start.45 = (s32[4]{0:T(128)S(1)}, s32[4]{0:T(128)}, u32[]{:S(2)}) copy-start(s32[4]{0:T(128)} %param.14) | copy-start | bytes 52
  104.4 8.9 %collective-permute-start.4 = (bf16[4,6,12,512]{3,2,1,0:T(8,128)(2,1)}, bf16[4,6,12,512]{3,2,1,0:T(8,128)(2,1)S(1)}, u32[]{:S(2)}, u32[]{:S(2)}) collective-permute-start(bf16[4,6,12,512]{3,2,1,0:T(8,128)(2,1)} %reshape.323), channel_id=1, source_target_pairs={{0,96},{32,0},{64,32},{96,64},{1,97},{33,1},{65,33},{97,65},{2,98}... | collective-permute-start | bytes 884744 | tf_op jit(solution)/shard_map/ppermute | solution.py:19
  113.4 22.0 %copy-start.7 = (bf16[4,12,12,512]{3,2,1,0:T(8,128)(2,1)}, bf16[4,12,12,512]{3,2,1,0:T(8,128)(2,1)S(1)}, u32[]{:S(2)}) copy-start(bf16[4,12,12,512]{3,2,1,0:T(8,128)(2,1)S(1)} %constant_dynamic-update-slice_fusion) | copy-start | bytes 1769476
  114.6 20.7 %collective-permute-start.5 = (bf16[4,12,12,512]{3,0,2,1:T(4,128)(2,1)}, bf16[4,12,12,512]{3,0,2,1:T(4,128)(2,1)}, u32[]{:S(2)}, u32[]{:S(2)}) collective-permute-start(bf16[4,12,12,512]{3,0,2,1:T(4,128)(2,1)} %copy.92), channel_id=1, source_target_pairs={{0,31},{1,0},{2,1},{3,2},{4,3},{5,4},{6,5},{7,6},{8,7},{9,8},{10,9... | collective-permute-start | bytes 1769480 | tf_op jit(solution)/shard_map/ppermute | solution.py:19
  154.2 8.8 %copy-start.35 = (bf16[288,2048]{1,0:T(8,128)(2,1)S(1)}, bf16[288,2048]{1,0:T(8,128)(2,1)}, u32[]{:S(2)}) copy-start(bf16[288,2048]{1,0:T(8,128)(2,1)} %copy-done.34) | copy-start | bytes 3538948
  156.6 5.5 %collective-permute-start.6 = (bf16[4,6,12,512]{3,2,1,0:T(8,128)(2,1)S(1)}, bf16[4,6,12,512]{3,2,1,0:T(8,128)(2,1)S(1)}, u32[]{:S(2)}, u32[]{:S(2)}) collective-permute-start(bf16[4,6,12,512]{3,2,1,0:T(8,128)(2,1)S(1)} %get-tuple-element.66), channel_id=1, source_target_pairs={{0,32},{32,64},{64,96},{96,0},{1,33},{33,65},{65,97},{97,1},{2,34}... | collective-permute-start | bytes 884744 | tf_op jit(solution)/shard_map/ppermute | solution.py:19
  162.7 17.4 %collective-permute-start.7 = (bf16[4,12,12,512]{3,0,2,1:T(4,128)(2,1)S(1)}, bf16[4,12,12,512]{3,0,2,1:T(4,128)(2,1)S(1)}, u32[]{:S(2)}, u32[]{:S(2)}) collective-permute-start(bf16[4,12,12,512]{3,0,2,1:T(4,128)(2,1)S(1)} %copy.96), channel_id=1, source_target_pairs={{0,1},{1,2},{2,3},{3,4},{4,5},{5,6},{6,7},{7,8},{8,9},{9,10},{10,1... | collective-permute-start | bytes 1769480 | tf_op jit(solution)/shard_map/ppermute | solution.py:19
  181.9 8.3 %copy-start.21 = (bf16[288,512]{1,0:T(8,128)(2,1)}, bf16[288,512]{1,0:T(8,128)(2,1)S(1)}, u32[]{:S(2)}) copy-start(bf16[288,512]{1,0:T(8,128)(2,1)S(1)} %reshape.328) | copy-start | bytes 884740
  208.0 14.5 %copy-start.9 = (bf16[2,2,1,6,1,12,1,8,64]{8,7,6,5,3,1,0,4,2:T(8,128)(2,1)S(1)}, bf16[2,2,1,6,1,12,1,8,64]{8,7,6,5,3,1,0,4,2:T(8,128)(2,1)}, u32[]{:S(2)}) copy-start(bf16[2,2,1,6,1,12,1,8,64]{8,7,6,5,3,1,0,4,2:T(8,128)(2,1)} %copy-done.8) | copy-start | bytes 884740
  240.2 11.9 %copy-start.29 = (bf16[4,6,12,512]{3,2,1,0:T(8,128)(2,1)S(1)}, bf16[4,6,12,512]{3,2,1,0:T(8,128)(2,1)}, u32[]{:S(2)}) copy-start(bf16[4,6,12,512]{3,2,1,0:T(8,128)(2,1)} %get-tuple-element.67) | copy-start | bytes 884740
  240.2 11.3 %collective-permute-start.8 = (bf16[4,6,12,512]{3,2,1,0:T(8,128)(2,1)S(1)}, bf16[4,6,12,512]{3,2,1,0:T(8,128)(2,1)S(1)}, u32[]{:S(2)}, u32[]{:S(2)}) collective-permute-start(bf16[4,6,12,512]{3,2,1,0:T(8,128)(2,1)S(1)} %reshape.330), channel_id=1, source_target_pairs={{0,96},{32,0},{64,32},{96,64},{1,97},{33,1},{65,33},{97,65},{2,98}... | collective-permute-start | bytes 884744 | tf_op jit(solution)/shard_map/ppermute | solution.py:19
  252.0 18.8 %collective-permute-start.9 = (bf16[4,12,12,512]{3,0,2,1:T(4,128)(2,1)S(1)}, bf16[4,12,12,512]{3,0,2,1:T(4,128)(2,1)S(1)}, u32[]{:S(2)}, u32[]{:S(2)}) collective-permute-start(bf16[4,12,12,512]{3,0,2,1:T(4,128)(2,1)S(1)} %copy.109), channel_id=1, source_target_pairs={{0,31},{1,0},{2,1},{3,2},{4,3},{5,4},{6,5},{7,6},{8,7},{9,8},{10,9... | collective-permute-start | bytes 1769480 | tf_op jit(solution)/shard_map/ppermute | solution.py:19
  (34 other events, 102.1 us)
Sparse Core Ops, SparseCore 0:
  238.2 176.6 all-reduce.3
where the time goes:
time: 438 us; the launch traced here: 433 us
  waiting for transfers between devices  138 us (32%)
  matrix products  67.1 us (15%)
  blocking collectives  67 us (15%)
  other arithmetic  53.2 us (12%)
  local copies, waits for them, and re-layouts  48.1 us (11%)
  between operations  45.6 us (10%)
  starting transfers between devices  13.6 us (3%)
    psum x1, waiting for transfers between devices, on_device(): lax.psum((grad_qkv, grad_out, grad_gain_attn, grad_up, grad_down, grad_ga...  73.9 us
    psum x1, blocking collectives, on_device(): lax.psum((grad_qkv, grad_out, grad_gain_attn, grad_up, grad_down, grad_ga...  67 us
    ppermute x10, waiting for transfers between devices, shifted(): lax.ppermute(value, axis, [(i, (i + by) % devices) for i in range(devices)])  64.1 us
    unnamed x103, local copies, waits for them, and re-layouts  18 us
    dot_general x1, matrix products, attend_back(): jnp.einsum('avbhcwne,aubgcxne->abcnvhwugx', dgrad, values, preferred_elem...  17.8 us
    convert_element_type x1, other arithmetic, attend_back(): grad_scores = (probs * (grad_probs - jnp.sum(grad_probs * probs, axis=-1,...  14.5 us
    ppermute x10, starting transfers between devices, shifted(): lax.ppermute(value, axis, [(i, (i + by) % devices) for i in range(devices)])  13.6 us
    reduce_sum x1, other arithmetic, attend(): probs = expo / jnp.sum(expo, axis=-1, keepdims=True)  12.6 us
  transfers between devices with their start and end apart: 11, of which 7 were waited for; matrix products, arithmetic and copies ran while one was open for 6% of the time, Pallas kernels for 0%

commit v1 on v0

v1 whole, which is shorter than its diff:
```python
import functools

import jax
import jax.numpy as jnp
from jax import lax
from jax.experimental import pallas as pl
from jax.experimental.pallas import tpu as pltpu
from jax.sharding import PartitionSpec as P

HEADS = 8
WV = 2
WH = 6
WW = 12
WIN = WV * WH * WW
PLANE = WH * WW
LABEL_ROWS = 80
LABELS = 128
EPS = 1e-05
MESH = pl.DeviceIdType.MESH
F32 = jnp.float32
BF16 = jnp.bfloat16
CUBE = 6
PART = 1024
WIDTH = 256
HALF = CUBE * PART
VMEM_BYTES = 60 * 1024 * 1024
DIMS_ZERO = (((0,), (0,)), ((), ()))
DIMS_LAST = (((1,), (1,)), ((), ()))


def mm(a, b):
    return jnp.dot(a, b, preferred_element_type=F32)


def mm_tn(a, b):
    return lax.dot_general(a, b, DIMS_ZERO, preferred_element_type=F32)


def mm_nt(a, b):
    return lax.dot_general(a, b, DIMS_LAST, preferred_element_type=F32)


def norm_stats(values):
    center = values - jnp.mean(values, axis=-1, keepdims=True)
    inv_scale = lax.rsqrt(jnp.mean(center * center, axis=-1, keepdims=True) + EPS)
    return (center * inv_scale, inv_scale)


def norm_back(grad, normed, inv_scale, gain):
    gain_grad = jnp.sum(grad * normed, axis=0, keepdims=True)
    graded = grad * gain
    term = inv_scale * (
        graded
        - jnp.mean(graded, axis=-1, keepdims=True)
        - normed * jnp.mean(graded * normed, axis=-1, keepdims=True)
    )
    return (term, gain_grad)


def wrap(value, count):
    return lax.rem(value + count, count)


def neighbours(step):
    lat, lon = lax.axis_index("lat"), lax.axis_index("lon")
    lats, lons = lax.axis_size("lat"), lax.axis_size("lon")
    lat_to, lon_to = wrap(lat + step, lats), wrap(lon + step, lons)
    return [(lat_to, lon), (lat, lon_to), (lat_to, lon_to)]


def cube_peers():
    lat, lon = lax.axis_index("lat"), lax.axis_index("lon")
    core, y_hi = lax.rem(lat, 2), lat // 2
    x, y_lo, z = lax.rem(lon, 4), lax.rem(lon // 4, 2), lon // 8
    y = y_hi * 2 + y_lo

    def device(x, y, z):
        return ((y // 2) * 2 + core, z * 8 + lax.rem(y, 2) * 4 + x)

    def flip(p):
        return p + 1 - 2 * lax.rem(p, 2)

    def first(p):
        return lax.rem(p + p // 2, 2)

    peers = [
        device(flip(x), y, z),
        device(3 - x, y, z),
        device(x, flip(y), z),
        device(x, 3 - y, z),
        device(x, y, flip(z)),
        device(x, y, 3 - z),
    ]
    bits = [first(x), x // 2, first(y), y // 2, first(z), z // 2]
    return (y_hi * 2 + 1 - core, lon), core, peers, bits


def greet(devices):
    barrier = pltpu.get_barrier_semaphore()
    for device in devices:
        pl.semaphore_signal(barrier, inc=1, device_id=device, device_id_type=MESH)
    pl.semaphore_wait(barrier, len(devices))


def remote(src, dst, send, recv, device):
    return pltpu.make_async_remote_copy(
        src_ref=src, dst_ref=dst, send_sem=send, recv_sem=recv, device_id=device, device_id_type=MESH
    )


def targets(window, row_ref, col_ref, sign):
    cell = lax.broadcasted_iota(jnp.int32, (WIN, 1), 0)
    level = (cell >= PLANE).astype(jnp.int32)
    inner = cell - PLANE * level
    row = jnp.floor((inner.astype(F32) + 0.5) * (1.0 / WW)).astype(jnp.int32)
    col = inner - WW * row
    down = jnp.where(level == 0, row_ref[2 * window], row_ref[2 * window + 1])
    across = jnp.where(level == 0, col_ref[2 * window], col_ref[2 * window + 1])
    row = row + sign * down
    col = col + sign * across
    if sign < 0:
        row_out, col_out = (row < 0).astype(jnp.int32), (col < 0).astype(jnp.int32)
    else:
        row_out, col_out = (row >= WH).astype(jnp.int32), (col >= WW).astype(jnp.int32)
    row = row - sign * WH * row_out
    col = col - sign * WW * col_out
    return row_out + 2 * col_out, row * WW + col, level


def one_hot(quadrant, index, which, width):
    lanes = lax.broadcasted_iota(jnp.int32, (index.shape[0], width), 1)
    return jnp.where((lanes == index) & (quadrant == which), 1.0, 0.0).astype(BF16)


def select(quadrant, index, sources):
    total = None
    for which, source in enumerate(sources):
        term = mm(one_hot(quadrant, index, which, source.shape[0]), source)
        total = term if total is None else total + term
    return total


def halo_in_kernel(tok, cot, lab, tok_x, cot_x, lab_x, send, recv):
    ahead = neighbours(1)
    greet(ahead + neighbours(-1))
    copies = []
    for a, (own, ext) in enumerate(((tok, tok_x), (lab, lab_x), (cot, cot_x))):
        for q in range(3):
            copies.append(remote(own, ext.at[q], send.at[a, q], recv.at[a, q], ahead[q]))
            copies[-1].start()
    for copy in copies:
        copy.wait()


def compute_kernel(
    rows, cols, tok, tok_x, cot, cot_x, lab, lab_x, gain_a, w_qkv, w_out, gain_m, w_up, w_down,
    grads, gains, out, grad_tok,
    tokf, cotf, labf, norm_a, h_a, qkv, probs, mixed, resid, norm_m, h_m, dh, dqkv,
):
    width = tok.shape[1]
    for w in range(2):
        here = pl.ds(w * WIN, WIN)
        quadrant, index, level = targets(w, rows, cols, -1)
        spread = index + PLANE * level
        tokf[here, :] = select(quadrant, spread, [tok[here, :]] + [tok_x[q, here, :] for q in range(3)])
        cotf[here, :] = select(
            quadrant, spread, [cot[here, :]] + [cot_x[q, here, :] for q in range(3)]
        ).astype(BF16)
        labf[here, :] = select(quadrant, index, [lab[...]] + [lab_x[q] for q in range(3)]).astype(BF16)
    normed, scale_a = norm_stats(tokf[...])
    norm_a[...] = normed
    h_a[...] = (normed * gain_a[...]).astype(BF16)
    for c in range(3):
        part = pl.ds(c * width, width)
        qkv[:, part] = mm(h_a[...], w_qkv[:, part]).astype(BF16)

    low = lax.broadcasted_iota(jnp.int32, (1, 128), 1) < 64

    def pair_stack(block):
        zero = jnp.zeros_like(block)
        return jnp.concatenate([jnp.where(low, block, zero), jnp.where(low, zero, block)], axis=0)

    def pair_join(stack):
        return jnp.where(low, stack[:WIN], stack[WIN:])

    for w in range(2):
        here = pl.ds(w * WIN, WIN)
        allowed = mm_nt(labf[here, :], labf[here, :]) > 0.5
        allowed = jnp.concatenate([allowed, allowed], axis=0)
        for p in range(HEADS // 2):
            lanes = [pl.ds(part * width + p * 128, 128) for part in range(3)]
            query = pair_stack(qkv[here, lanes[0]])
            scores = mm_nt(query, qkv[here, lanes[1]]) * 0.125
            scores = jnp.where(allowed, scores, -jnp.inf)
            expo = jnp.exp(scores - jnp.max(scores, axis=-1, keepdims=True))
            prob = expo * (1.0 / jnp.sum(expo, axis=-1, keepdims=True))
            probs[w * 4 + p] = prob
            mixed[here, pl.ds(p * 128, 128)] = pair_join(
                mm(prob.astype(BF16), qkv[here, lanes[2]])
            ).astype(BF16)

    attn = mm(mixed[...], w_out[...]).astype(BF16).astype(F32)
    resid[...] = tokf[...] + attn
    normed, scale_m = norm_stats(resid[...])
    norm_m[...] = normed
    h_m[...] = (normed * gain_m[...]).astype(BF16)
    dh[...] = jnp.zeros_like(dh)

    def ff_step(c, carry):
        part = pl.ds(pl.multiple_of(c * 512, 512), 512)
        pre = mm(h_m[...], w_up[:, part])
        cdf = 0.5 * (1.0 + lax.erf(pre * 0.7071067811865476))
        act = (pre * cdf).astype(BF16)
        slope = cdf + pre * jnp.exp(-0.5 * pre * pre) * 0.3989422804014327
        resid[...] += mm(act, w_down[part, :])
        grad_pre = (mm_nt(cotf[...], w_down[part, :]) * slope).astype(BF16)
        dh[...] += mm_nt(grad_pre, w_up[:, part])
        down = mm_tn(act, cotf[...]).astype(BF16)
        up = mm_tn(h_m[...], grad_pre).astype(BF16)
        for b in range(2):
            cut = slice(b * WIDTH, (b + 1) * WIDTH)
            grads[pl.ds(pl.multiple_of(b * 2048 + c * 512, 512), 512), :] = down[:, cut]
            grads[pl.ds(pl.multiple_of(4096 + (2 * c + b) * 512, 512), 512), :] = up[:, cut]
        return carry

    lax.fori_loop(0, 4, ff_step, 0)
    out[...] = resid[...].astype(BF16)
    term, gain_grad_m = norm_back(dh[...], norm_m[...], scale_m, gain_m[...])
    resid[...] = cotf[...].astype(F32) + term
    grad_attn = resid[...].astype(BF16)
    grad_out = mm_tn(mixed[...], grad_attn).astype(BF16)
    for b in range(2):
        grads[pl.ds(8192 + b * 512, 512), :] = grad_out[:, b * WIDTH : (b + 1) * WIDTH]
    mixed[...] = mm_nt(grad_attn, w_out[...]).astype(BF16)

    for w in range(2):
        here = pl.ds(w * WIN, WIN)
        for p in range(HEADS // 2):
            lanes = [pl.ds(part * width + p * 128, 128) for part in range(3)]
            prob = probs[w * 4 + p]
            dmix = pair_stack(mixed[here, pl.ds(p * 128, 128)])
            query = pair_stack(qkv[here, lanes[0]])
            dprob = mm_nt(dmix, qkv[here, lanes[2]])
            dqkv[here, lanes[2]] = mm_tn(prob.astype(BF16), dmix).astype(BF16)
            dscore = prob * (dprob - jnp.sum(dprob * prob, axis=-1, keepdims=True)) * 0.125
            dscore = dscore.astype(BF16)
            dqkv[here, lanes[0]] = pair_join(mm(dscore, qkv[here, lanes[1]])).astype(BF16)
            dqkv[here, lanes[1]] = mm_tn(dscore, query).astype(BF16)

    dframe = None
    for c in range(3):
        part = pl.ds(c * width, width)
        grad_qkv = mm_tn(h_a[...], dqkv[:, part]).astype(BF16)
        for b in range(2):
            grads[pl.ds(9216 + (2 * c + b) * 512, 512), :] = grad_qkv[:, b * WIDTH : (b + 1) * WIDTH]
        term = mm_nt(dqkv[:, part], w_qkv[:, part])
        dframe = term if dframe is None else dframe + term
    dframe = dframe.astype(BF16).astype(F32)
    term, gain_grad_a = norm_back(dframe, norm_a[...], scale_a, gain_a[...])
    grad_tok[...] = (resid[...] + term).astype(BF16)
    for r in range(4):
        gains[r : r + 1, :] = gain_grad_a[:, r * 128 : (r + 1) * 128]
        gains[r + 4 : r + 5, :] = gain_grad_m[:, r * 128 : (r + 1) * 128]


def reduce_kernel(
    grads, gains, out, grad_tok,
    total, gains_sum, out_x, grad_tok_x,
    mine, core_in, cube_in, gains_acc, gains_in,
    halo_send, halo_recv, core_send, core_recv, rs_send, rs_recv, ag_send, ag_recv, end_send, end_recv,
    gain_send, gain_recv,
):
    core_peer, core, peers, bits = cube_peers()
    back = neighbours(-1)
    greet([core_peer] + peers + back + neighbours(1))
    started = []

    def go(*args):
        copy = remote(*args)
        copy.start()
        started.append(copy)
        return copy

    def rows_of(half, p, offset, count):
        return pl.ds(pl.multiple_of(half * HALF + p * PART + offset, 16), count)

    core_copies = [
        go(grads.at[rows_of(1 - core, p, 0, PART)], core_in.at[p], core_send.at[p], core_recv.at[p], core_peer)
        for p in range(CUBE)
    ]
    gain_peers = [core_peer] + peers

    def gain_go(step):
        return go(
            gains_acc.at[step], gains_in.at[step], gain_send.at[step], gain_recv.at[step], gain_peers[step]
        )

    gains_acc[0] = gains[...]
    gain_copies = [gain_go(0)]

    def gain_next():
        step = len(gain_copies)
        gain_copies[-1].wait_recv()
        summed = gains_acc[step - 1] + gains_in[step - 1]
        if step < 7:
            gains_acc[step] = summed
            gain_copies.append(gain_go(step))
        else:
            gains_sum[...] = summed

    offsets = [0] * CUBE
    rs_copies = {}

    def rs_go(p, s):
        dim, count = (p + s) % CUBE, PART >> (s + 1)
        rs_copies[p, s] = go(
            mine.at[p, pl.ds(pl.multiple_of(offsets[p] + (1 - bits[dim]) * count, 16), count)],
            cube_in.at[p, pl.ds(PART - (PART >> s), count)],
            rs_send.at[p, s],
            rs_recv.at[p, s],
            peers[dim],
        )
        offsets[p] = offsets[p] + bits[dim] * count

    for p in range(CUBE):
        core_copies[p].wait_recv()
        mine[p] = (grads[rows_of(core, p, 0, PART), :].astype(F32) + core_in[p].astype(F32)).astype(BF16)
        rs_go(p, 0)
    gain_next()
    halo_copies = []
    for a, (own, ext) in enumerate(((out, out_x), (grad_tok, grad_tok_x))):
        for q in range(3):
            halo_copies.append(go(own, ext.at[q], halo_send.at[a, q], halo_recv.at[a, q], back[q]))

    ag_copies = {}

    def ag_go(p, s):
        dim, count = (p + s) % CUBE, PART >> (s + 1)
        place = total.at[rows_of(core, p, offsets[p], count)]
        ag_copies[p, s] = go(place, place, ag_send.at[p, s], ag_recv.at[p, s], peers[dim])
        offsets[p] = offsets[p] - bits[dim] * count

    for s in range(CUBE):
        count = PART >> (s + 1)
        for p in range(CUBE):
            rs_copies[p, s].wait_recv()
            here = pl.ds(pl.multiple_of(offsets[p], 16), count)
            arrived = cube_in[p, pl.ds(PART - (PART >> s), count), :].astype(F32)
            summed = (mine[p, here, :].astype(F32) + arrived).astype(BF16)
            if s < CUBE - 1:
                mine[p, here, :] = summed
                rs_go(p, s + 1)
            else:
                total[rows_of(core, p, offsets[p], count), :] = summed
                ag_go(p, s)
        gain_next()

    end_copies = []
    for s in reversed(range(CUBE)):
        for p in range(CUBE):
            ag_copies[p, s].wait_recv()
            if s > 0:
                ag_go(p, s - 1)
            else:
                place = total.at[rows_of(core, p, 0, PART)]
                end_copies.append(go(place, place, end_send.at[p], end_recv.at[p], core_peer))
    for copy in end_copies + halo_copies:
        copy.wait_recv()
    for copy in started:
        copy.wait_send()


def finish_kernel(
    rows, cols, total, gains, out, out_x, grad_tok, grad_tok_x,
    block_out, grad_tokens, gain_a, gain_m, grad_qkv, grad_out, grad_up, grad_down,
    stage, sems,
):
    moves = []

    def put(start, count, target):
        stage[pl.ds(start, count), :] = total[pl.ds(start, count), :].astype(F32)
        move = pltpu.make_async_copy(stage.at[pl.ds(start, count)], target, sems.at[len(moves)])
        move.start()
        moves.append(move)

    for b in range(2):
        for r in range(4):
            put(b * 2048 + r * 512, 512, grad_down.at[pl.ds(r * 512, 512), pl.ds(b * WIDTH, WIDTH)])
    for b in range(8):
        put(4096 + b * 512, 512, grad_up.at[:, pl.ds(b * WIDTH, WIDTH)])
    for b in range(2):
        put(8192 + b * 512, 512, grad_out.at[:, pl.ds(b * WIDTH, WIDTH)])
    for b in range(6):
        put(9216 + b * 512, 512, grad_qkv.at[:, pl.ds(b * WIDTH, WIDTH)])
    for w in range(2):
        here = pl.ds(w * WIN, WIN)
        quadrant, index, level = targets(w, rows, cols, 1)
        spread = index + PLANE * level
        for own, ext, result in ((out, out_x, block_out), (grad_tok, grad_tok_x, grad_tokens)):
            result[here, :] = select(
                quadrant, spread, [own[here, :]] + [ext[q, here, :] for q in range(3)]
            ).astype(BF16)
    for r in range(4):
        gain_a[:, r * 128 : (r + 1) * 128] = gains[r : r + 1, :]
        gain_m[:, r * 128 : (r + 1) * 128] = gains[r + 4 : r + 5, :]
    for move in moves:
        move.wait()


VMEM = pl.BlockSpec(memory_space=pltpu.VMEM)
SMEM = pl.BlockSpec(memory_space=pltpu.SMEM)
ANY = pl.BlockSpec(memory_space=pl.ANY)
DMA = pltpu.SemaphoreType.DMA


def call(kernel, outs, in_specs, out_specs, scratch, name, collective_id=None):
    params = {"vmem_limit_bytes": VMEM_BYTES}
    if collective_id is not None:
        params.update(collective_id=collective_id, has_side_effects=True)
    return pl.pallas_call(
        kernel,
        out_shape=[jax.ShapeDtypeStruct(shape, dtype) for shape, dtype in outs],
        in_specs=in_specs,
        out_specs=out_specs,
        scratch_shapes=scratch,
        compiler_params=pltpu.CompilerParams(**params),
        name=name,
    )


def on_device(
    tokens,
    region_ids,
    shift_lat,
    shift_lon,
    gain_attn,
    w_qkv,
    w_out,
    gain_mlp,
    w_up,
    w_down,
    cotangent,
):
    levels, lat_rows, lon_cols, width = tokens.shape
    cells = levels * lat_rows * lon_cols
    ff = w_up.shape[1]
    tok = tokens.reshape(cells, width)
    cot = cotangent.reshape(cells, width)
    lab = (region_ids.reshape(-1, 1) == jnp.arange(LABELS)[None, :]).astype(BF16)
    lab = jnp.pad(lab, ((0, LABEL_ROWS - PLANE), (0, 0)))
    gain_a, gain_m = gain_attn.reshape(1, width), gain_mlp.reshape(1, width)

    tile = ((cells, width), BF16)
    halo = ((3, cells, width), BF16)
    tok_x, cot_x, lab_x = call(
        halo_in_kernel,
        [halo, halo, ((3, LABEL_ROWS, LABELS), BF16)],
        [VMEM] * 3,
        [VMEM] * 3,
        [DMA((3, 3)), DMA((3, 3))],
        "halo_in",
        0,
    )(tok, cot, lab)

    grads, gains, out, grad_tok = call(
        compute_kernel,
        [((2 * HALF, WIDTH), BF16), ((8, 128), F32), tile, tile],
        [SMEM, SMEM] + [VMEM] * 12,
        [VMEM] * 4,
        [
            pltpu.VMEM((cells, width), F32),
            pltpu.VMEM((cells, width), BF16),
            pltpu.VMEM((cells, LABELS), BF16),
            pltpu.VMEM((cells, width), F32),
            pltpu.VMEM((cells, width), BF16),
            pltpu.VMEM((cells, 3 * width), BF16),
            pltpu.VMEM((8, 2 * WIN, WIN), F32),
            pltpu.VMEM((cells, width), BF16),
            pltpu.VMEM((cells, width), F32),
            pltpu.VMEM((cells, width), F32),
            pltpu.VMEM((cells, width), BF16),
            pltpu.VMEM((cells, width), F32),
            pltpu.VMEM((cells, 3 * width), BF16),
        ],
        "block",
    )(shift_lat, shift_lon, tok, tok_x, cot, cot_x, lab, lab_x, gain_a, w_qkv, w_out, gain_m, w_up, w_down)

    total, gains_sum, out_x, grad_tok_x = call(
        reduce_kernel,
        [((2 * HALF, WIDTH), BF16), ((8, 128), F32), halo, halo],
        [VMEM] * 4,
        [VMEM] * 4,
        [
            pltpu.VMEM((CUBE, PART, WIDTH), BF16),
            pltpu.VMEM((CUBE, PART, WIDTH), BF16),
            pltpu.VMEM((CUBE, PART, WIDTH), BF16),
            pltpu.VMEM((7, 8, 128), F32),
            pltpu.VMEM((7, 8, 128), F32),
            DMA((2, 3)),
            DMA((2, 3)),
            DMA((CUBE,)),
            DMA((CUBE,)),
            DMA((CUBE, CUBE)),
            DMA((CUBE, CUBE)),
            DMA((CUBE, CUBE)),
            DMA((CUBE, CUBE)),
            DMA((CUBE,)),
            DMA((CUBE,)),
            DMA((7,)),
            DMA((7,)),
        ],
        "reduce",
        1,
    )(grads, gains, out, grad_tok)

    results = call(
        finish_kernel,
        [
            tile,
            tile,
            ((1, width), F32),
            ((1, width), F32),
            ((width, 3 * width), F32),
            ((width, width), F32),
            ((width, ff), F32),
            ((ff, width), F32),
        ],
        [SMEM, SMEM] + [VMEM] * 6,
        [VMEM] * 4 + [ANY] * 4,
        [pltpu.VMEM((2 * HALF, WIDTH), F32), DMA((24,))],
        "finish",
    )(shift_lat, shift_lon, total, gains_sum, out, out_x, grad_tok, grad_tok_x)
    block_out, grad_tokens, grad_gain_attn, grad_gain_mlp, grad_qkv, grad_out, grad_up, grad_down = results
    return (
        block_out.reshape(tokens.shape),
        grad_tokens.reshape(tokens.shape),
        grad_gain_attn.reshape(width),
        grad_qkv,
        grad_out,
        grad_gain_mlp.reshape(width),
        grad_up,
        grad_down,
    )


def solution(mesh):
    placed = (
        P(None, "lat", "lon", None),
        P("lat", "lon"),
        P(),
        P(),
        P(),
        P(),
        P(),
        P(),
        P(),
        P(),
        P(None, "lat", "lon", None),
    )
    return jax.shard_map(
        on_device,
        mesh=mesh,
        in_specs=placed,
        out_specs=(
            P(None, "lat", "lon", None),
            P(None, "lat", "lon", None),
            P(),
            P(),
            P(),
            P(),
            P(),
            P(),
        ),
        check_vma=False,
    )
```

time: 438 us -> 174 us (0.40); the launches traced: 433 us -> 174 us
  Pallas kernels: 0 us -> 164 us
  waiting for transfers between devices: 138 us -> 0 us
  matrix products: 67.1 us -> 0 us
  blocking collectives: 67 us -> 0 us
  other arithmetic: 53.2 us -> 0.69 us
  between operations: 45.6 us -> 0.69 us
  local copies, waits for them, and re-layouts: 48.1 us -> 8.33 us
  starting transfers between devices: 13.6 us -> 0 us
    pallas_call x0 -> x4, Pallas kernels: none -> 164 us  [the longest x1 92.5 us: on_device(): call(reduce_kernel, [((2 * HALF, WIDTH), BF16), ((8, 128), F32), halo, ha...]
    psum x1 -> x0, waiting for transfers between devices: 73.9 us -> none  [on_device(): lax.psum((grad_qkv, grad_out, grad_gain_attn, grad_up, grad_down, grad_ga...]
    dot_general x18 -> x0, matrix products: 67.1 us -> none  [the longest x1 17.8 us: attend_back(): jnp.einsum('avbhcwne,aubgcxne->abcnvhwugx', dgrad, values, preferred_elem...]
    psum x1 -> x0, blocking collectives: 67 us -> none  [on_device(): lax.psum((grad_qkv, grad_out, grad_gain_attn, grad_up, grad_down, grad_ga...]
    ppermute x10 -> x0, waiting for transfers between devices: 64.1 us -> none  [shifted(): lax.ppermute(value, axis, [(i, (i + by) % devices) for i in range(devices)])]
    convert_element_type x7 -> x0, other arithmetic: 31 us -> none  [the longest x1 14.5 us: attend_back(): grad_scores = (probs * (grad_probs - jnp.sum(grad_probs * probs, axis=-1,...]
    reduce_sum x7 -> x0, other arithmetic: 17.8 us -> none  [the longest x1 12.6 us: attend(): probs = expo / jnp.sum(expo, axis=-1, keepdims=True)]
    unnamed x103 -> x4, local copies, waits for them, and re-layouts: 18 us -> 3.94 us
  transfers between devices with their start and end apart: 11 -> 0, of which waited for: 7 -> 0; matrix products, arithmetic and copies ran while one was open for 6% -> 0% of each run, Pallas kernels for 0% -> 0%
where the time goes in v1:
time: 174 us
  Pallas kernels  164 us (94%)
  local copies, waits for them, and re-layouts  8.33 us (5%)
    pallas_call x1, Pallas kernels, on_device(): call(reduce_kernel, [((2 * HALF, WIDTH), BF16), ((8, 128), F32), halo, ha...  92.5 us
    pallas_call x1, Pallas kernels, on_device(): call(halo_in_kernel, [halo, halo, ((3, LABEL_ROWS, LABELS), BF16)], [VMEM...  40.3 us
    pallas_call x1, Pallas kernels, on_device(): call(compute_kernel, [((2 * HALF, WIDTH), BF16), ((8, 128), F32), tile, t...  21.4 us
    pallas_call x1, Pallas kernels, on_device(): call(finish_kernel, [tile, tile, ((1, width), F32), ((1, width), F32), ((...  9.66 us
    unnamed x4, local copies, waits for them, and re-layouts  3.94 us

profile of v1, /device:TPU:1, one launch (start us, length us, event | category | flops | bytes accessed | tf_op | source)
XLA Modules:
  0.0 173.6 jit_solution(1610651310225532643)
XLA Ops:
  0.6 0.8 eq.15
  1.4 0.1 iota_compare_fusion
  1.5 0.6 pad_convert_fusion.lab
  2.1 1.0 copy.23
  3.1 0.8 reshape.42.tok
  3.9 1.0 copy.24
  4.9 0.8 reshape.43.cot
  5.7 40.3 %halo_in.1 = (bf16[3,288,512]{2,1,0:T(8,128)(2,1)}, bf16[3,288,512]{2,1,0:T(8,128)(2,1)}, bf16[3,80,128]{2,1,0:T(8,128)(2,1)}) custom-call(bf16[288,512]{1,0:T(8,128)(2,1)} %reshape.42.tok, bf16[288,512]{1,0:T(8,128)(2,1)} %reshape.43.cot, bf16[80,128]{1,0:T(8,128)(2,1)} %pad_convert_fusion.lab), custom_call_target="tpu_custom_call" | custom-call | tf_op jit(solution)/shard_map/halo_in/pallas_call | solution.py:455
  46.1 21.4 %block.1 = (bf16[12288,256]{1,0:T(8,128)(2,1)}, f32[8,128]{1,0:T(8,128)}, bf16[288,512]{1,0:T(8,128)(2,1)}, bf16[288,512]{1,0:T(8,128)(2,1)}) custom-call(s32[4]{0:T(128)} %rows.3, s32[4]{0:T(128)} %cols.3, bf16[288,512]{1,0:T(8,128)(2,1)} %reshape.42.tok, bf16[3,288,512]{2,1,0:T(8,128)(2,1)} %get-tuple-element.27.tok_x, bf16[288,512]{1,0:T(8,128)(2,1)} %reshape.43.cot, ...), custom_call_target="tpu_custom_call" | custom-call | tf_op jit(solution)/shard_map/block/pallas_call | solution.py:465
  67.4 92.5 %reduce.1 = (bf16[12288,256]{1,0:T(8,128)(2,1)}, f32[8,128]{1,0:T(8,128)}, bf16[3,288,512]{2,1,0:T(8,128)(2,1)}, bf16[3,288,512]{2,1,0:T(8,128)(2,1)}) custom-call(bf16[12288,256]{1,0:T(8,128)(2,1)} %get-tuple-element.30.grads, f32[8,128]{1,0:T(8,128)} %get-tuple-element.31.gains, bf16[288,512]{1,0:T(8,128)(2,1)} %get-tuple-element.32.out, ...), custom_call_target="tpu_custom_call" | custom-call | tf_op jit(solution)/shard_map/reduce/pallas_call | solution.py:488
  159.9 9.7 %finish.1 = (bf16[288,512]{1,0:T(8,128)(2,1)}, bf16[288,512]{1,0:T(8,128)(2,1)}, f32[1,512]{1,0:T(1,128)}, f32[1,512]{1,0:T(1,128)}, f32[512,1536]{1,0:T(8,128)}...) custom-call(s32[4]{0:T(128)} %rows.3, s32[4]{0:T(128)} %cols.3, ...), custom_call_target="tpu_custom_call" | custom-call | tf_op jit(solution)/shard_map/finish/pallas_call | solution.py:516
  169.6 1.0 reshape.46
  170.6 0.9 copy.25
  171.6 1.0 reshape.47
  172.6 0.9 copy.26

commit v2 on v1

v2 whole, which is shorter than its diff:
```python
import functools

import jax
import jax.numpy as jnp
from jax import lax
from jax.experimental import pallas as pl
from jax.experimental.pallas import tpu as pltpu
from jax.sharding import PartitionSpec as P

HEADS = 8
WV = 2
WH = 6
WW = 12
WIN = WV * WH * WW
PLANE = WH * WW
LANES = 128
PAD = 16
SIDE = 4
EPS = 1e-05
MESH = pl.DeviceIdType.MESH
F32 = jnp.float32
BF16 = jnp.bfloat16
CHUNKS = 4
PART = 1024
ROUNDS = (256, 64, 16)
SEMS = 20
VMEM_BYTES = 60 * 1024 * 1024
DIMS_ZERO = (((0,), (0,)), ((), ()))
DIMS_LAST = (((1,), (1,)), ((), ()))


def mm(a, b):
    return jnp.dot(a, b, preferred_element_type=F32)


def mm_tn(a, b):
    return lax.dot_general(a, b, DIMS_ZERO, preferred_element_type=F32)


def mm_nt(a, b):
    return lax.dot_general(a, b, DIMS_LAST, preferred_element_type=F32)


def norm_stats(values):
    center = values - jnp.mean(values, axis=-1, keepdims=True)
    inv_scale = lax.rsqrt(jnp.mean(center * center, axis=-1, keepdims=True) + EPS)
    return (center * inv_scale, inv_scale)


def norm_back(grad, normed, inv_scale, gain):
    gain_grad = jnp.sum(grad * normed, axis=0, keepdims=True)
    graded = grad * gain
    term = inv_scale * (
        graded
        - jnp.mean(graded, axis=-1, keepdims=True)
        - normed * jnp.mean(graded * normed, axis=-1, keepdims=True)
    )
    return (term, gain_grad)


def places():
    lat, lon = lax.axis_index("lat"), lax.axis_index("lon")
    lats, lons = lax.axis_size("lat"), lax.axis_size("lon")
    core, y_hi = lax.rem(lat, 2), lat // 2
    x, y_lo, z = lax.rem(lon, SIDE), lax.rem(lon // SIDE, 2), lon // (2 * SIDE)
    y = y_hi * 2 + y_lo

    def device(x, y, z):
        x, y, z = lax.rem(x, SIDE), lax.rem(y, SIDE), lax.rem(z, SIDE)
        return ((y // 2) * 2 + core, z * 2 * SIDE + lax.rem(y, 2) * SIDE + x)

    steps = range(1, SIDE)
    peers = [
        [device(x + j, y, z) for j in steps],
        [device(x, y + j, z) for j in steps],
        [device(x, y, z + j) for j in steps],
    ]
    grid = {
        "below": (lax.rem(lat + 1, lats), lon),
        "above": (lax.rem(lat + lats - 1, lats), lon),
        "right": (lat, lax.rem(lon + 1, lons)),
        "left": (lat, lax.rem(lon + lons - 1, lons)),
    }
    return grid, core, (y_hi * 2 + 1 - core, lon), peers, (x, y, z)


def remote(src, dst, send, recv, device):
    return pltpu.make_async_remote_copy(
        src_ref=src, dst_ref=dst, send_sem=send, recv_sem=recv, device_id=device, device_id_type=MESH
    )


def cell_places(count, pad):
    cell = lax.broadcasted_iota(jnp.int32, (count, 1), 0)
    plane = WH * pad
    level = (cell >= plane).astype(jnp.int32)
    inner = cell - plane * level
    row = jnp.floor((inner.astype(F32) + 0.5) * (1.0 / pad)).astype(jnp.int32)
    return level, row, inner - pad * row


def per_level(level, ref, window):
    return jnp.where(level == 0, ref[2 * window], ref[2 * window + 1])


def fold(value, limit):
    out = ((value < 0) | (value >= limit)).astype(jnp.int32)
    return jnp.where(value < 0, value + limit, jnp.where(value >= limit, value - limit, value)), out


def one_hot(hit, index, width):
    lanes = lax.broadcasted_iota(jnp.int32, (index.shape[0], width), 1)
    return jnp.where((lanes == index) & hit, 1.0, 0.0).astype(BF16)


def roll_pair(level, row, col, out):
    index = level * PLANE + row * WW + col
    return one_hot(out == 0, index, WIN), one_hot(out == 1, index, WIN)


def row_roll(window, ref, sign, pad=WW):
    level, row, col = cell_places(WV * WH * pad, pad)
    row, out = fold(row + sign * per_level(level, ref, window), WH)
    return roll_pair(level, row, col, jnp.where(col < WW, out, 2))


def col_roll(window, ref, sign):
    level, row, col = cell_places(WIN, WW)
    col, out = fold(col + sign * per_level(level, ref, window), WW)
    return roll_pair(level, row, col, out)


def pack_matrix():
    level, row, col = cell_places(WIN, WW)
    return one_hot(level >= 0, (level * WH + row) * PAD + col, WV * WH * PAD)


def apply_roll(pair, here, there):
    return (mm(pair[0], here) + mm(pair[1], there)).astype(BF16)


def block_kernel(
    rows, cols, tok_in, cot_in, ids_in, gain_a, gain_m, w_qkv_hbm, w_out_hbm, w_up_hbm, w_down_hbm,
    total_a_hbm, total_b_hbm, gains_sum, out_t, out_tx, tok_t, tok_tx,
    w_qkv, w_out, w_up, w_down, padded,
    tok, tok_above, tok_rows, tok_left, cot, cot_above, cot_rows, cot_left, ids, ids_x,
    cotf, tokf, labf, norm_a, h_a, qkv, probs, mixed, resid, norm_m, h_m, dh, dqkv,
    out_f, out_right, tok_f, tok_right, gains_acc, gains_in,
    ga, core_a, mine_a, r1_a, m1_a, r2_a, m2_a, r3_a, total_a,
    gb, core_b, mine_b, r1_b, m1_b, r2_b, m2_b, r3_b, total_b,
    load_sem, halo_send, halo_recv, sum_send, sum_recv, gain_send, gain_recv, store_sem,
):
    width = gain_a.shape[1]
    grid, core, core_peer, peers, position = places()
    loads = [
        pltpu.make_async_copy(src, dst, load_sem.at[k])
        for k, (src, dst) in enumerate(
            ((w_qkv_hbm, w_qkv), (w_out_hbm, w_out), (w_up_hbm, w_up), (w_down_hbm, w_down))
        )
    ]
    for load in loads:
        load.start()
    greeted = [core_peer] + [p for axis in peers for p in axis] + list(grid.values())
    barrier = pltpu.get_barrier_semaphore()
    for device in greeted:
        pl.semaphore_signal(barrier, inc=1, device_id=device, device_id_type=MESH)

    started = []
    stores = []

    def go(*args):
        copy = remote(*args)
        copy.start()
        started.append(copy)
        return copy

    halos = []

    def halo_go(src, dst, device):
        k = len(halos)
        halos.append(go(src, dst, halo_send.at[k], halo_recv.at[k], device))
        return halos[-1]

    def window(w):
        return pl.ds(w * WIN, WIN)

    padded[...] = jnp.zeros_like(padded)
    packer = pack_matrix()
    for source, packed in ((tok_in, tok), (cot_in, cot)):
        for g in range(source.shape[0]):
            padded[pl.ds(g * PAD, WW), :] = source[g]
        for w in range(2):
            span = WV * WH * PAD
            packed[window(w), :] = mm(packer, padded[pl.ds(w * span, span), :]).astype(BF16)
    ids[0:8, :] = jnp.zeros((8, LANES), jnp.int32)
    ids[0:WH, 0:WW] = ids_in[...]
    pl.semaphore_wait(barrier, len(greeted))
    lat_tok = [halo_go(tok.at[window(w)], tok_above.at[window(w)], grid["below"]) for w in range(2)]
    lat_ids = halo_go(ids.at[pl.ds(0, 8)], ids.at[pl.ds(8, 8)], grid["below"])
    lat_cot = [halo_go(cot.at[window(w)], cot_above.at[window(w)], grid["below"]) for w in range(2)]
    row_pairs = [row_roll(w, rows, -1) for w in range(2)]
    col_pairs = [col_roll(w, cols, -1) for w in range(2)]
    lon_tok, lon_cot = [], []
    for w in range(2):
        lat_tok[w].wait_recv()
        tok_rows[window(w), :] = apply_roll(row_pairs[w], tok[window(w), :], tok_above[window(w), :])
        lon_tok.append(halo_go(tok_rows.at[window(w)], tok_left.at[window(w)], grid["right"]))
        if w == 0:
            lat_ids.wait_recv()
            lon_ids = halo_go(ids, ids_x, grid["right"])
    for w in range(2):
        lat_cot[w].wait_recv()
        cot_rows[window(w), :] = apply_roll(row_pairs[w], cot[window(w), :], cot_above[window(w), :])
        lon_cot.append(halo_go(cot_rows.at[window(w)], cot_left.at[window(w)], grid["right"]))

    lon_ids.wait_recv()
    ids_all = jnp.concatenate([ids[...], ids_x[...]], axis=0).astype(F32).astype(BF16)
    for load in loads:
        load.wait()
    for w in range(2):
        level, row, col = cell_places(WIN, WW)
        row, row_out = fold(row - per_level(level, rows, w), WH)
        col, col_out = fold(col - per_level(level, cols, w), WW)
        picked = mm(one_hot(level >= 0, (row_out + 2 * col_out) * 8 + row, 32), ids_all)
        lanes = lax.broadcasted_iota(jnp.int32, (WIN, LANES), 1)
        label = jnp.sum(jnp.where(lanes == col, picked, 0.0), axis=-1, keepdims=True)
        labf[window(w), :] = jnp.where(lanes.astype(F32) == label, 1.0, 0.0).astype(BF16)
    for w in range(2):
        lon_tok[w].wait_recv()
        tokf[window(w), :] = apply_roll(
            col_pairs[w], tok_rows[window(w), :], tok_left[window(w), :]
        ).astype(F32)
    normed, scale_a = norm_stats(tokf[...])
    norm_a[...] = normed
    h_a[...] = (normed * gain_a[...]).astype(BF16)
    for c in range(3):
        part = pl.ds(c * width, width)
        qkv[:, part] = mm(h_a[...], w_qkv[:, part]).astype(BF16)

    low = lax.broadcasted_iota(jnp.int32, (1, LANES), 1) < LANES // 2

    def pair_stack(block):
        zero = jnp.zeros_like(block)
        return jnp.concatenate([jnp.where(low, block, zero), jnp.where(low, zero, block)], axis=0)

    def pair_join(stack):
        return jnp.where(low, stack[:WIN], stack[WIN:])

    def pair_lanes(p):
        return [pl.ds(part * width + p * LANES, LANES) for part in range(3)]

    for w in range(2):
        here = window(w)
        allowed = mm_nt(labf[here, :], labf[here, :]) > 0.5
        allowed = jnp.concatenate([allowed, allowed], axis=0)
        for p in range(HEADS // 2):
            lanes = pair_lanes(p)
            query = pair_stack(qkv[here, lanes[0]])
            scores = mm_nt(query, qkv[here, lanes[1]]) * 0.125
            scores = jnp.where(allowed, scores, -jnp.inf)
            expo = jnp.exp(scores - jnp.max(scores, axis=-1, keepdims=True))
            prob = expo * (1.0 / jnp.sum(expo, axis=-1, keepdims=True))
            probs[w * 4 + p] = prob
            mixed[here, pl.ds(p * LANES, LANES)] = pair_join(
                mm(prob.astype(BF16), qkv[here, lanes[2]])
            ).astype(BF16)

    attn = mm(mixed[...], w_out[...]).astype(BF16).astype(F32)
    resid[...] = tokf[...] + attn
    normed, scale_m = norm_stats(resid[...])
    norm_m[...] = normed
    h_m[...] = (normed * gain_m[...]).astype(BF16)
    dh[...] = jnp.zeros_like(dh)
    for w in range(2):
        lon_cot[w].wait_recv()
        cotf[window(w), :] = apply_roll(col_pairs[w], cot_rows[window(w), :], cot_left[window(w), :])

    set_a = (ga, core_a, mine_a, (r1_a, r2_a, r3_a), (mine_a, m1_a, m2_a), total_a, total_a_hbm)
    set_b = (gb, core_b, mine_b, (r1_b, r2_b, r3_b), (mine_b, m1_b, m2_b), total_b, total_b_hbm)

    def block(offset, count):
        return pl.ds(pl.multiple_of(offset, 16), count)

    def store(src, dst):
        copy = pltpu.make_async_copy(src, dst, store_sem.at[len(stores)])
        copy.start()
        stores.append(copy)

    def chain(refs, i, k):
        partial, core_in, mine, arrivals, sums, total, total_hbm = refs
        order = [(k + r) % 3 for r in range(3)]
        used = [0]

        def send(src, dst, device):
            n = used[0]
            used[0] += 1
            return go(src, dst, sum_send.at[k, n], sum_recv.at[k, n], device)

        first = send(partial.at[1 - core, i], core_in.at[i], core_peer)
        yield
        first.wait_recv()
        mine[i] = (partial[core, i].astype(F32) + core_in[i].astype(F32)).astype(BF16)
        offset, offsets = 0, []
        for r, count in enumerate(ROUNDS):
            at = position[order[r]]
            copies = [
                send(
                    sums[r].at[i, block(lax.rem(at + j, SIDE) * count, count)],
                    arrivals[r].at[i, j - 1],
                    peers[order[r]][j - 1],
                )
                for j in range(1, SIDE)
            ]
            yield
            for copy in copies:
                copy.wait_recv()
            summed = sums[r][i, block(at * count, count), :].astype(F32)
            for j in range(SIDE - 1):
                summed = summed + arrivals[r][i, j].astype(F32)
            offset = offset + at * count
            offsets.append(offset)
            if r < 2:
                sums[r + 1][i] = summed.astype(BF16)
            else:
                total[core, i, block(offset, count), :] = summed.astype(BF16)
        for r in reversed(range(3)):
            place = total.at[core, i, block(offsets[r], ROUNDS[r])]
            copies = [send(place, place, peers[order[r]][j]) for j in range(SIDE - 1)]
            yield
            for copy in copies:
                copy.wait_recv()
        last = send(total.at[core, i], total.at[core, i], core_peer)
        store(total.at[core, i], total_hbm.at[core, i])
        yield
        last.wait_recv()
        store(total.at[1 - core, i], total_hbm.at[1 - core, i])

    def gain_chain():
        used = [0]

        def send(src, device):
            n = used[0]
            used[0] += 1
            return go(src, gains_in.at[n], gain_send.at[n], gain_recv.at[n], device)

        copy = send(gains_acc.at[0], core_peer)
        yield
        copy.wait_recv()
        gains_acc[1] = gains_acc[0] + gains_in[0]
        for axis in range(3):
            copies = [send(gains_acc.at[axis + 1], peer) for peer in peers[axis]]
            yield
            for copy in copies:
                copy.wait_recv()
            base = 1 + 3 * axis
            summed = (gains_acc[axis + 1] + gains_in[base + 1]) + (gains_in[base] + gains_in[base + 2])
            if axis < 2:
                gains_acc[axis + 2] = summed
            else:
                gains_sum[...] = summed

    def advance(*chains):
        for link in chains:
            next(link, None)

    chains = [chain(set_a, i, i) for i in range(CHUNKS)] + [chain(set_b, i, CHUNKS + i) for i in range(CHUNKS)]

    for c in range(CHUNKS):
        part = pl.ds(c * 512, 512)
        pre = mm(h_m[...], w_up[:, part])
        cdf = 0.5 * (1.0 + lax.erf(pre * 0.7071067811865476))
        act = (pre * cdf).astype(BF16)
        slope = cdf + pre * jnp.exp(-0.5 * pre * pre) * 0.3989422804014327
        resid[...] += mm(act, w_down[part, :])
        grad_pre = (mm_nt(cotf[...], w_down[part, :]) * slope).astype(BF16)
        dh[...] += mm_nt(grad_pre, w_up[:, part])
        down = mm_tn(act, cotf[...]).astype(BF16)
        up = mm_tn(h_m[...], grad_pre).astype(BF16)
        for b in range(2):
            cut = slice(b * 256, (b + 1) * 256)
            ga[0, c, b * 512 : (b + 1) * 512, :] = down[:, cut]
            ga[1, c, b * 512 : (b + 1) * 512, :] = up[:, cut]
        advance(chains[c])
        if c > 0:
            advance(chains[c - 1])
    out_f[...] = resid[...].astype(BF16)
    out_lon = halo_go(out_f, out_right, grid["left"])
    term, gain_grad_m = norm_back(dh[...], norm_m[...], scale_m, gain_m[...])
    resid[...] = cotf[...].astype(F32) + term
    grad_attn = resid[...].astype(BF16)

    def put(half, i, b, value):
        for j in range(2):
            gb[half, i, j * 512 : (j + 1) * 512, :] = value[:, b + j * LANES : b + (j + 1) * LANES]

    grad_out = mm_tn(mixed[...], grad_attn).astype(BF16)
    put(0, 0, 0, grad_out)
    put(1, 0, 256, grad_out)
    advance(chains[4], chains[3])
    mixed[...] = mm_nt(grad_attn, w_out[...]).astype(BF16)

    homes = {(0, 0): (0, 1), (1, 0): (1, 1), (2, 0): (0, 2), (0, 1): (1, 2), (1, 1): (0, 3), (2, 1): (1, 3)}
    pump = [[0, 1, 4], [2, 3], [0, 1, 4, 2], [3, 0, 1]]
    for p in range(HEADS // 2):
        lanes = pair_lanes(p)
        for w in range(2):
            here = window(w)
            prob = probs[w * 4 + p]
            dmix = pair_stack(mixed[here, pl.ds(p * LANES, LANES)])
            query = pair_stack(qkv[here, lanes[0]])
            dprob = mm_nt(dmix, qkv[here, lanes[2]])
            dqkv[here, lanes[2]] = mm_tn(prob.astype(BF16), dmix).astype(BF16)
            dscore = prob * (dprob - jnp.sum(dprob * prob, axis=-1, keepdims=True)) * 0.125
            dscore = dscore.astype(BF16)
            dqkv[here, lanes[0]] = pair_join(mm(dscore, qkv[here, lanes[1]])).astype(BF16)
            dqkv[here, lanes[1]] = mm_tn(dscore, query).astype(BF16)
        if p % 2 == 1:
            for c in range(3):
                half, i = homes[c, p // 2]
                cut = pl.ds(c * width + (p // 2) * 256, 256)
                put(half, i, 0, mm_tn(h_a[...], dqkv[:, cut]).astype(BF16))
            if p == 1:
                advance(chains[5])
            else:
                advance(chains[6], chains[7])
        advance(*[chains[k] for k in pump[p]])

    dframe = None
    for c in range(3):
        part = pl.ds(c * width, width)
        term = mm_nt(dqkv[:, part], w_qkv[:, part])
        dframe = term if dframe is None else dframe + term
    dframe = dframe.astype(BF16).astype(F32)
    advance(chains[5], chains[6], chains[7])
    term, gain_grad_a = norm_back(dframe, norm_a[...], scale_a, gain_a[...])
    for r in range(4):
        cut = slice(r * LANES, (r + 1) * LANES)
        gains_acc[0, r : r + 1, :] = gain_grad_a[:, cut]
        gains_acc[0, r + 4 : r + 5, :] = gain_grad_m[:, cut]
    gains_link = gain_chain()
    advance(gains_link)
    tok_f[...] = (resid[...] + term).astype(BF16)
    tok_lon = halo_go(tok_f, tok_right, grid["left"])
    back_pairs = [col_roll(w, cols, 1) for w in range(2)]

    def turn(arrived, own, other, rolled, rolled_x):
        arrived.wait_recv()
        for w in range(2):
            here = window(w)
            rolled[here, :] = apply_roll(back_pairs[w], own[here, :], other[here, :])
        return halo_go(rolled, rolled_x, grid["above"])

    out_lat = turn(out_lon, out_f, out_right, out_t, out_tx)
    chains.append(gains_link)
    tok_lat = None
    for step in range(9):
        advance(*chains)
        if step == 1:
            tok_lat = turn(tok_lon, tok_f, tok_right, tok_t, tok_tx)
    for copy in (out_lat, tok_lat):
        copy.wait_recv()
    for copy in started:
        copy.wait_send()
    for copy in stores:
        copy.wait()


def finish_kernel(
    rows, cols, total_a_hbm, total_b_hbm, gains, out_t, out_tx, tok_t, tok_tx,
    block_out, grad_tokens, gain_a, gain_m, grad_qkv, grad_out, grad_up, grad_down,
    total_a, total_b, stage_a, stage_b, in_sems, out_sems,
):
    loads, moves = {}, []
    for i in range(CHUNKS):
        for half in range(2):
            for kind, (src, dst) in enumerate(((total_a_hbm, total_a), (total_b_hbm, total_b))):
                load = pltpu.make_async_copy(src.at[half, i], dst.at[half, i], in_sems.at[kind, half, i])
                load.start()
                loads[kind, half, i] = load

    def put(stage, total, half, i, b, target):
        stage[half, i, b * 512 : (b + 1) * 512, :] = total[half, i, b * 512 : (b + 1) * 512, :].astype(F32)
        move = pltpu.make_async_copy(
            stage.at[half, i, pl.ds(b * 512, 512)], target, out_sems.at[len(moves)]
        )
        move.start()
        moves.append(move)

    homes = {(0, 0): None, (1, 0): None, (0, 1): (0, 0), (1, 1): (1, 0), (0, 2): (2, 0), (1, 2): (0, 1), (0, 3): (1, 1), (1, 3): (2, 1)}
    for i in range(CHUNKS):
        for half in range(2):
            loads[0, half, i].wait()
            for b in range(2):
                if half == 0:
                    target = grad_down.at[pl.ds(i * 512, 512), pl.ds(b * 256, 256)]
                else:
                    target = grad_up.at[:, pl.ds(i * 512 + b * 256, 256)]
                put(stage_a, total_a, half, i, b, target)
            loads[1, half, i].wait()
            for b in range(2):
                if i == 0:
                    target = grad_out.at[:, pl.ds(half * 256 + b * LANES, LANES)]
                else:
                    c, second = homes[half, i]
                    target = grad_qkv.at[:, pl.ds(c * 512 + second * 256 + b * LANES, LANES)]
                put(stage_b, total_b, half, i, b, target)
    for w in range(2):
        here = pl.ds(w * WIN, WIN)
        pair = row_roll(w, rows, 1, PAD)
        for own, other, result in ((out_t, out_tx, block_out), (tok_t, tok_tx, grad_tokens)):
            rolled = apply_roll(pair, own[here, :], other[here, :])
            for g in range(WV * WH):
                result[w * WV * WH + g] = rolled[g * PAD : g * PAD + WW]
    for r in range(4):
        cut = slice(r * LANES, (r + 1) * LANES)
        gain_a[:, cut] = gains[r : r + 1, :]
        gain_m[:, cut] = gains[r + 4 : r + 5, :]
    for move in moves:
        move.wait()


VMEM = pl.BlockSpec(memory_space=pltpu.VMEM)
SMEM = pl.BlockSpec(memory_space=pltpu.SMEM)
ANY = pl.BlockSpec(memory_space=pl.ANY)
DMA = pltpu.SemaphoreType.DMA


def call(kernel, outs, in_specs, out_specs, scratch, name, collective_id=None):
    params = {"vmem_limit_bytes": VMEM_BYTES}
    if collective_id is not None:
        params.update(collective_id=collective_id, has_side_effects=True)
    return pl.pallas_call(
        kernel,
        out_shape=[jax.ShapeDtypeStruct(shape, dtype) for shape, dtype in outs],
        in_specs=in_specs,
        out_specs=out_specs,
        scratch_shapes=scratch,
        compiler_params=pltpu.CompilerParams(**params),
        name=name,
    )


def sum_buffers(lanes):
    shapes = [(2, CHUNKS, PART, lanes), (CHUNKS, PART, lanes), (CHUNKS, PART, lanes)]
    for r, count in enumerate(ROUNDS):
        shapes.append((CHUNKS, SIDE - 1, count, lanes))
        if r < 2:
            shapes.append((CHUNKS, count, lanes))
    shapes.append((2, CHUNKS, PART, lanes))
    return [pltpu.VMEM(shape, BF16) for shape in shapes]


def on_device(
    tokens,
    region_ids,
    shift_lat,
    shift_lon,
    gain_attn,
    w_qkv,
    w_out,
    gain_mlp,
    w_up,
    w_down,
    cotangent,
):
    levels, lat_rows, lon_cols, width = tokens.shape
    cells = levels * lat_rows * lon_cols
    ff = w_up.shape[1]
    lines = (levels * lat_rows, lon_cols, width)
    tile = ((cells, width), BF16)
    half, full = pltpu.VMEM((cells, width), BF16), pltpu.VMEM((cells, width), F32)
    total_a, total_b, gains_sum, out_t, out_tx, tok_t, tok_tx = call(
        block_kernel,
        [((2, CHUNKS, PART, 256), BF16), ((2, CHUNKS, PART, LANES), BF16), ((8, LANES), F32)] + [tile] * 4,
        [SMEM] * 2 + [VMEM] * 5 + [ANY] * 4,
        [ANY] * 2 + [VMEM] * 5,
        [pltpu.VMEM(w.shape, BF16) for w in (w_qkv, w_out, w_up, w_down)]
        + [pltpu.VMEM((lines[0] * PAD, width), BF16)]
        + [half] * 8
        + [pltpu.VMEM((16, LANES), jnp.int32)] * 2
        + [
            half,
            full,
            pltpu.VMEM((cells, LANES), BF16),
            full,
            half,
            pltpu.VMEM((cells, 3 * width), BF16),
            pltpu.VMEM((HEADS, 2 * WIN, WIN), F32),
            half,
            full,
            full,
            half,
            full,
            pltpu.VMEM((cells, 3 * width), BF16),
        ]
        + [half] * 4
        + [pltpu.VMEM((4, 8, LANES), F32), pltpu.VMEM((10, 8, LANES), F32)]
        + sum_buffers(256)
        + sum_buffers(LANES)
        + [
            DMA((4,)),
            DMA((14,)),
            DMA((14,)),
            DMA((2 * CHUNKS, SEMS)),
            DMA((2 * CHUNKS, SEMS)),
            DMA((10,)),
            DMA((10,)),
            DMA((4 * CHUNKS,)),
        ],
        "block",
        0,
    )(
        shift_lat, shift_lon, tokens.reshape(lines), cotangent.reshape(lines), region_ids,
        gain_attn.reshape(1, width), gain_mlp.reshape(1, width), w_qkv, w_out, w_up, w_down,
    )
    results = call(
        finish_kernel,
        [
            (lines, BF16),
            (lines, BF16),
            ((1, width), F32),
            ((1, width), F32),
            ((width, 3 * width), F32),
            ((width, width), F32),
            ((width, ff), F32),
            ((ff, width), F32),
        ],
        [SMEM] * 2 + [ANY] * 2 + [VMEM] * 5,
        [VMEM] * 4 + [ANY] * 4,
        [
            pltpu.VMEM((2, CHUNKS, PART, 256), BF16),
            pltpu.VMEM((2, CHUNKS, PART, LANES), BF16),
            pltpu.VMEM((2, CHUNKS, PART, 256), F32),
            pltpu.VMEM((2, CHUNKS, PART, LANES), F32),
            DMA((2, 2, CHUNKS)),
            DMA((8 * CHUNKS,)),
        ],
        "finish",
    )(shift_lat, shift_lon, total_a, total_b, gains_sum, out_t, out_tx, tok_t, tok_tx)
    block_out, grad_tokens, grad_gain_attn, grad_gain_mlp, grad_qkv, grad_out, grad_up, grad_down = results
    return (
        block_out.reshape(tokens.shape),
        grad_tokens.reshape(tokens.shape),
        grad_gain_attn.reshape(width),
        grad_qkv,
        grad_out,
        grad_gain_mlp.reshape(width),
        grad_up,
        grad_down,
    )


def solution(mesh):
    placed = (
        P(None, "lat", "lon", None),
        P("lat", "lon"),
        P(),
        P(),
        P(),
        P(),
        P(),
        P(),
        P(),
        P(),
        P(None, "lat", "lon", None),
    )
    return jax.shard_map(
        on_device,
        mesh=mesh,
        in_specs=placed,
        out_specs=(
            P(None, "lat", "lon", None),
            P(None, "lat", "lon", None),
            P(),
            P(),
            P(),
            P(),
            P(),
            P(),
        ),
        check_vma=False,
    )
```

time: 174 us -> 134 us (0.77)
  Pallas kernels: 164 us -> 126 us
    pallas_call x4 -> x2, Pallas kernels: 164 us -> 126 us  [the longest x1 117 us: on_device(): call(block_kernel, [((2, CHUNKS, PART, 256), BF16), ((2, CHUNKS, PART, LA...]
    reshape x4 -> x0, local copies, waits for them, and re-layouts: 3.62 us -> none  [the longest x1 1.03 us: on_device(): block_out.reshape(tokens.shape)]
    unnamed x4, local copies, waits for them, and re-layouts: 3.94 us -> 7.44 us
where the time goes in v2:
time: 134 us
  Pallas kernels  126 us (94%)
  local copies, waits for them, and re-layouts  7.44 us (6%)
    pallas_call x1, Pallas kernels, on_device(): call(block_kernel, [((2, CHUNKS, PART, 256), BF16), ((2, CHUNKS, PART, LA...  117 us
    pallas_call x1, Pallas kernels, on_device(): call(finish_kernel, [(lines, BF16), (lines, BF16), ((1, width), F32), ((1...  8.56 us
    unnamed x4, local copies, waits for them, and re-layouts  7.44 us

profile of v2, /device:TPU:1, one launch (start us, length us, event | category | flops | bytes accessed | tf_op | source)
XLA Modules:
  0.0 134.1 jit_solution(16365020293648800231)
XLA Ops:
  0.6 1.8 %copy.19 = bf16[4,6,12,512]{3,2,1,0:T(8,128)(2,1)} copy(bf16[4,6,12,512]{3,0,2,1:T(4,128)(2,1)} %param.11) | data formatting | bytes 589824 | tf_op args[0]
  2.4 1.8 %copy.20 = bf16[4,6,12,512]{3,2,1,0:T(8,128)(2,1)} copy(bf16[4,6,12,512]{3,0,2,1:T(4,128)(2,1)} %param.21) | data formatting | bytes 589824 | tf_op args[10]
  4.2 117.4 %block.1 = (bf16[2,4,1024,256]{3,2,1,0:T(8,128)(2,1)}, bf16[2,4,1024,128]{3,2,1,0:T(8,128)(2,1)}, f32[8,128]{1,0:T(8,128)}, bf16[288,512]{1,0:T(8,128)(2,1)}, bf...) custom-call(s32[4]{0:T(128)} %rows.3, s32[4]{0:T(128)} %cols.3, ...), custom_call_target="tpu_custom_call" | custom-call | tf_op jit(solution)/shard_map/block/pallas_call | solution.py:572
  121.6 8.6 %finish.1 = (bf16[24,12,512]{2,1,0:T(8,128)(2,1)}, bf16[24,12,512]{2,1,0:T(8,128)(2,1)}, f32[1,512]{1,0:T(1,128)}, f32[1,512]{1,0:T(1,128)}, f32[512,1536]{1,0:T...) custom-call(s32[4]{0:T(128)} %rows.3, s32[4]{0:T(128)} %cols.3, ...), custom_call_target="tpu_custom_call" | custom-call | tf_op jit(solution)/shard_map/finish/pallas_call | solution.py:616
  130.2 1.9 %copy.21 = bf16[4,6,12,512]{3,0,2,1:T(4,128)(2,1)} copy(bf16[4,6,12,512]{3,2,1,0:T(8,128)(2,1)} %bitcast.11) | data formatting | bytes 589824
  132.2 1.9 %copy.22 = bf16[4,6,12,512]{3,0,2,1:T(4,128)(2,1)} copy(bf16[4,6,12,512]{3,2,1,0:T(8,128)(2,1)} %bitcast.10) | data formatting | bytes 589824

commit v3 on v2

v3 whole, which is shorter than its diff:
```python
import functools

import jax
import jax.numpy as jnp
from jax import lax
from jax.experimental import pallas as pl
from jax.experimental.pallas import tpu as pltpu
from jax.sharding import PartitionSpec as P

HEADS = 8
WV = 2
WH = 6
WW = 12
WIN = WV * WH * WW
PLANE = WH * WW
LANES = 128
LEVELS = 4
CELLS = LEVELS * PLANE
SIDE = 4
EPS = 1e-05
MESH = pl.DeviceIdType.MESH
F32 = jnp.float32
BF16 = jnp.bfloat16
CHUNKS = 4
CHAINS = 12
PART = 1024
ROUNDS = (256, 64, 16)
SEMS = 20
VMEM_BYTES = 60 * 1024 * 1024
DIMS_ZERO = (((0,), (0,)), ((), ()))
DIMS_LAST = (((1,), (1,)), ((), ()))


def mm(a, b):
    return jnp.dot(a, b, preferred_element_type=F32)


def mm_tn(a, b):
    return lax.dot_general(a, b, DIMS_ZERO, preferred_element_type=F32)


def mm_nt(a, b):
    return lax.dot_general(a, b, DIMS_LAST, preferred_element_type=F32)


def norm_stats(values):
    center = values - jnp.mean(values, axis=-1, keepdims=True)
    inv_scale = lax.rsqrt(jnp.mean(center * center, axis=-1, keepdims=True) + EPS)
    return (center * inv_scale, inv_scale)


def norm_back(grad, normed, inv_scale, gain):
    gain_grad = jnp.sum(grad * normed, axis=0, keepdims=True)
    graded = grad * gain
    term = inv_scale * (
        graded
        - jnp.mean(graded, axis=-1, keepdims=True)
        - normed * jnp.mean(graded * normed, axis=-1, keepdims=True)
    )
    return (term, gain_grad)


def places():
    lat, lon = lax.axis_index("lat"), lax.axis_index("lon")
    lats, lons = lax.axis_size("lat"), lax.axis_size("lon")
    core, y_hi = lax.rem(lat, 2), lat // 2
    x, y_lo, z = lax.rem(lon, SIDE), lax.rem(lon // SIDE, 2), lon // (2 * SIDE)
    y = y_hi * 2 + y_lo

    def device(x, y, z):
        x, y, z = lax.rem(x, SIDE), lax.rem(y, SIDE), lax.rem(z, SIDE)
        return ((y // 2) * 2 + core, z * 2 * SIDE + lax.rem(y, 2) * SIDE + x)

    steps = range(1, SIDE)
    peers = [
        [device(x + j, y, z) for j in steps],
        [device(x, y + j, z) for j in steps],
        [device(x, y, z + j) for j in steps],
    ]
    grid = {
        "below": (lax.rem(lat + 1, lats), lon),
        "above": (lax.rem(lat + lats - 1, lats), lon),
        "right": (lat, lax.rem(lon + 1, lons)),
        "left": (lat, lax.rem(lon + lons - 1, lons)),
    }
    return grid, core, (y_hi * 2 + 1 - core, lon), peers, (x, y, z)


def remote(src, dst, send, recv, device):
    return pltpu.make_async_remote_copy(
        src_ref=src, dst_ref=dst, send_sem=send, recv_sem=recv, device_id=device, device_id_type=MESH
    )


def div(value, by):
    return jnp.floor((value.astype(F32) + 0.5) * (1.0 / by)).astype(jnp.int32)


def frame_cells(start, count):
    cell = start + lax.broadcasted_iota(jnp.int32, (count, 1), 0)
    level = div(cell, PLANE)
    row = div(cell - level * PLANE, WW)
    return level, row, cell - level * PLANE - row * WW


def data_cells():
    cell = lax.broadcasted_iota(jnp.int32, (CELLS, 1), 0)
    spot = div(cell, LEVELS)
    row = div(spot, WW)
    return cell - spot * LEVELS, row, spot - row * WW


def row_cells():
    cell = lax.broadcasted_iota(jnp.int32, (CELLS, 1), 0)
    row = div(cell, LEVELS * WW)
    level = div(cell - row * LEVELS * WW, WW)
    return level, row, cell - row * LEVELS * WW - level * WW


def per_level(level, ref):
    value = ref[LEVELS - 1]
    for k in reversed(range(LEVELS - 1)):
        value = jnp.where(level == k, ref[k], value)
    return value


def fold(value, limit):
    out = ((value < 0) | (value >= limit)).astype(jnp.int32)
    return jnp.where(value < 0, value + limit, jnp.where(value >= limit, value - limit, value)), out


def one_hot(hit, index, width):
    lanes = lax.broadcasted_iota(jnp.int32, (index.shape[0], width), 1)
    return jnp.where((lanes == index) & hit, 1.0, 0.0).astype(BF16)


def roll_pair(index, out, width):
    return one_hot(out == 0, index, width), one_hot(out == 1, index, width)


def apply_roll(pair, here, there):
    return (mm(pair[0], here) + mm(pair[1], there)).astype(BF16)


def block_kernel(
    rows, cols, tok_in, cot_in, ids_in, gain_a, gain_m, w_qkv_hbm, w_out_hbm, w_up_hbm, w_down_hbm,
    total_hbm, gains_sum, out_t, out_tx, tok_t, tok_tx,
    w_qkv, w_out, w_up, w_down,
    tok_above, cot_above, tok_rows, tok_left, cot_rows, cot_left, ids, ids_x,
    cotf, tokf, labf, norm_a, h_a, qkv, probs, mixed, resid, norm_m, h_m, dh, dqkv,
    out_f, out_right, tok_f, tok_right, gains_acc, gains_in,
    partial, core_in, mine, r1, m1, r2, m2, r3, total,
    load_sem, halo_send, halo_recv, sum_send, sum_recv, gain_send, gain_recv, store_sem,
):
    width = gain_a.shape[1]
    grid, core, core_peer, peers, position = places()
    loads = [
        pltpu.make_async_copy(src, dst, load_sem.at[k])
        for k, (src, dst) in enumerate(
            ((w_qkv_hbm, w_qkv), (w_out_hbm, w_out), (w_up_hbm, w_up), (w_down_hbm, w_down))
        )
    ]
    greeted = [core_peer] + [p for axis in peers for p in axis] + list(grid.values())
    barrier = pltpu.get_barrier_semaphore()
    for device in greeted:
        pl.semaphore_signal(barrier, inc=1, device_id=device, device_id_type=MESH)
    for load in loads:
        load.start()

    started = []
    stores = []

    def go(*args):
        copy = remote(*args)
        copy.start()
        started.append(copy)
        return copy

    halos = []

    def halo_go(src, dst, device):
        k = len(halos)
        halos.append(go(src, dst, halo_send.at[k], halo_recv.at[k], device))
        return halos[-1]

    def window(w):
        return pl.ds(w * WIN, WIN)

    ids[0:8, :] = jnp.zeros((8, LANES), jnp.int32)
    ids[0:WH, 0:WW] = ids_in[...]
    for above in (tok_above, cot_above):
        above[0:WW] = jnp.zeros((WW, LEVELS, width), BF16)
    used_rows = pl.ds(WW, PLANE - WW)
    pl.semaphore_wait(barrier, len(greeted))
    lat_tok = halo_go(tok_in.at[used_rows], tok_above.at[used_rows], grid["below"])
    lat_ids = halo_go(ids.at[pl.ds(0, 8)], ids.at[pl.ds(8, 8)], grid["below"])
    lat_cot = halo_go(cot_in.at[used_rows], cot_above.at[used_rows], grid["below"])
    level, row, col = frame_cells(0, CELLS)
    row, row_out = fold(row - per_level(level, rows), WH)
    row_pair = roll_pair((row * WW + col) * LEVELS + level, row_out, CELLS)
    level, row, col = frame_cells(0, CELLS)
    col, col_out = fold(col - per_level(level, cols), WW)
    col_index = lax.rem(level, WV) * PLANE + row * WW + col
    col_pairs = [
        roll_pair(col_index[w * WIN : (w + 1) * WIN], col_out[w * WIN : (w + 1) * WIN], WIN) for w in range(2)
    ]
    lat_tok.wait_recv()
    tok_rows[...] = apply_roll(
        row_pair, tok_in[...].reshape(CELLS, width), tok_above[...].reshape(CELLS, width)
    )
    lon_tok = [halo_go(tok_rows.at[window(w)], tok_left.at[window(w)], grid["right"]) for w in range(2)]
    lat_ids.wait_recv()
    lon_ids = halo_go(ids, ids_x, grid["right"])
    lat_cot.wait_recv()
    cot_rows[...] = apply_roll(
        row_pair, cot_in[...].reshape(CELLS, width), cot_above[...].reshape(CELLS, width)
    )
    lon_cot = []

    def lon_cot_go(w):
        lon_cot.append(halo_go(cot_rows.at[window(w)], cot_left.at[window(w)], grid["right"]))

    lon_ids.wait_recv()
    ids_all = jnp.concatenate([ids[...], ids_x[...]], axis=0).astype(F32).astype(BF16)
    level, row, col = frame_cells(0, CELLS)
    row, row_out = fold(row - per_level(level, rows), WH)
    col, col_out = fold(col - per_level(level, cols), WW)
    picked = mm(one_hot(level >= 0, (row_out + 2 * col_out) * 8 + row, 32), ids_all)
    lanes = lax.broadcasted_iota(jnp.int32, (CELLS, LANES), 1)
    label = jnp.sum(jnp.where(lanes == col, picked, 0.0), axis=-1, keepdims=True)
    labf[...] = jnp.where(lanes.astype(F32) == label, 1.0, 0.0).astype(BF16)
    scale_a = []

    def forward_in(w):
        here = window(w)
        lon_tok[w].wait_recv()
        lon_cot_go(w)
        values = apply_roll(col_pairs[w], tok_rows[here, :], tok_left[here, :]).astype(F32)
        tokf[here, :] = values
        normed, scale = norm_stats(values)
        scale_a.append(scale)
        norm_a[here, :] = normed
        h_a[here, :] = (normed * gain_a[...]).astype(BF16)
        if w == 0:
            loads[0].wait()
        for c in range(3):
            part = pl.ds(c * width, width)
            qkv[here, part] = mm(h_a[here, :], w_qkv[:, part]).astype(BF16)

    low = lax.broadcasted_iota(jnp.int32, (1, LANES), 1) < LANES // 2

    def pair_stack(block):
        zero = jnp.zeros_like(block)
        return jnp.concatenate([jnp.where(low, block, zero), jnp.where(low, zero, block)], axis=0)

    def pair_join(stack):
        return jnp.where(low, stack[:WIN], stack[WIN:])

    def pair_lanes(p):
        return [pl.ds(part * width + p * LANES, LANES) for part in range(3)]

    for w in range(2):
        here = window(w)
        forward_in(w)
        allowed = mm_nt(labf[here, :], labf[here, :]) > 0.5
        allowed = jnp.concatenate([allowed, allowed], axis=0)
        for p in range(HEADS // 2):
            lanes = pair_lanes(p)
            query = pair_stack(qkv[here, lanes[0]])
            scores = mm_nt(query, qkv[here, lanes[1]]) * 0.125
            scores = jnp.where(allowed, scores, -jnp.inf)
            expo = jnp.exp(scores - jnp.max(scores, axis=-1, keepdims=True))
            prob = expo * (1.0 / jnp.sum(expo, axis=-1, keepdims=True))
            probs[w * 4 + p] = prob
            mixed[here, pl.ds(p * LANES, LANES)] = pair_join(
                mm(prob.astype(BF16), qkv[here, lanes[2]])
            ).astype(BF16)

    for load in loads[1:]:
        load.wait()
    attn = mm(mixed[...], w_out[...]).astype(BF16).astype(F32)
    resid[...] = tokf[...] + attn
    normed, scale_m = norm_stats(resid[...])
    norm_m[...] = normed
    h_m[...] = (normed * gain_m[...]).astype(BF16)
    dh[...] = jnp.zeros_like(dh)
    for w in range(2):
        lon_cot[w].wait_recv()
        cotf[window(w), :] = apply_roll(col_pairs[w], cot_rows[window(w), :], cot_left[window(w), :])

    arrivals, sums = (r1, r2, r3), (mine, m1, m2)

    def block(offset, count):
        return pl.ds(pl.multiple_of(offset, 16), count)

    def store(src, dst):
        copy = pltpu.make_async_copy(src, dst, store_sem.at[len(stores)])
        copy.start()
        stores.append(copy)

    def chain(i):
        order = [(i + r) % 3 for r in range(3)]
        used = [0]

        def send(src, dst, device):
            n = used[0]
            used[0] += 1
            return go(src, dst, sum_send.at[i, n], sum_recv.at[i, n], device)

        first = send(partial.at[1 - core, i], core_in.at[i], core_peer)
        yield
        first.wait_recv()
        mine[i] = (partial[core, i].astype(F32) + core_in[i].astype(F32)).astype(BF16)
        offset, offsets = 0, []
        for r, count in enumerate(ROUNDS):
            at = position[order[r]]
            copies = [
                send(
                    sums[r].at[i, block(lax.rem(at + j, SIDE) * count, count)],
                    arrivals[r].at[i, j - 1],
                    peers[order[r]][j - 1],
                )
                for j in range(1, SIDE)
            ]
            yield
            for copy in copies:
                copy.wait_recv()
            summed = sums[r][i, block(at * count, count), :].astype(F32)
            for j in range(SIDE - 1):
                summed = summed + arrivals[r][i, j].astype(F32)
            offset = offset + at * count
            offsets.append(offset)
            if r < 2:
                sums[r + 1][i] = summed.astype(BF16)
            else:
                total[core, i, block(offset, count), :] = summed.astype(BF16)
        for r in reversed(range(3)):
            place = total.at[core, i, block(offsets[r], ROUNDS[r])]
            copies = [send(place, place, peers[order[r]][j]) for j in range(SIDE - 1)]
            yield
            for copy in copies:
                copy.wait_recv()
        last = send(total.at[core, i], total.at[core, i], core_peer)
        store(total.at[core, i], total_hbm.at[core, i])
        yield
        last.wait_recv()
        store(total.at[1 - core, i], total_hbm.at[1 - core, i])

    def gain_chain():
        used = [0]

        def send(src, device):
            n = used[0]
            used[0] += 1
            return go(src, gains_in.at[n], gain_send.at[n], gain_recv.at[n], device)

        copy = send(gains_acc.at[0], core_peer)
        yield
        copy.wait_recv()
        gains_acc[1] = gains_acc[0] + gains_in[0]
        for axis in range(3):
            copies = [send(gains_acc.at[axis + 1], peer) for peer in peers[axis]]
            yield
            for copy in copies:
                copy.wait_recv()
            base = 1 + 3 * axis
            summed = (gains_acc[axis + 1] + gains_in[base + 1]) + (gains_in[base] + gains_in[base + 2])
            if axis < 2:
                gains_acc[axis + 2] = summed
            else:
                gains_sum[...] = summed

    def advance(*chains):
        for link in chains:
            next(link, None)

    chains = [chain(i) for i in range(CHAINS)]

    def step(*which):
        for i in which:
            next(chains[i], None)

    for c in range(CHUNKS):
        part = pl.ds(c * 512, 512)
        pre = mm(h_m[...], w_up[:, part])
        cdf = 0.5 * (1.0 + lax.erf(pre * 0.7071067811865476))
        act = (pre * cdf).astype(BF16)
        slope = cdf + pre * jnp.exp(-0.5 * pre * pre) * 0.3989422804014327
        resid[...] += mm(act, w_down[part, :])
        grad_pre = (mm_nt(cotf[...], w_down[part, :]) * slope).astype(BF16)
        dh[...] += mm_nt(grad_pre, w_up[:, part])
        down = mm_tn(act, cotf[...]).astype(BF16)
        up = mm_tn(h_m[...], grad_pre).astype(BF16)
        for b in range(4):
            spot = slice((b % 2) * 512, (b % 2 + 1) * 512)
            cut = slice(b * LANES, (b + 1) * LANES)
            partial[0, 2 * c + b // 2, spot, :] = down[:, cut]
            partial[1, 2 * c + b // 2, spot, :] = up[:, cut]
        step(2 * c, 2 * c + 1)
        if c > 0:
            step(2 * c - 2, 2 * c - 1)
    out_f[...] = resid[...].astype(BF16)
    out_lon = halo_go(out_f, out_right, grid["left"])
    term, gain_grad_m = norm_back(dh[...], norm_m[...], scale_m, gain_m[...])
    resid[...] = cotf[...].astype(F32) + term
    grad_attn = resid[...].astype(BF16)

    def put(half, i, b, value):
        for j in range(2):
            partial[half, 8 + i, j * 512 : (j + 1) * 512, :] = value[:, b + j * LANES : b + (j + 1) * LANES]

    grad_out = mm_tn(mixed[...], grad_attn).astype(BF16)
    put(0, 0, 0, grad_out)
    put(1, 0, 256, grad_out)
    step(8, 6, 7)
    mixed[...] = mm_nt(grad_attn, w_out[...]).astype(BF16)
    step(0, 1)

    homes = {(0, 0): (0, 1), (1, 0): (1, 1), (2, 0): (0, 2), (0, 1): (1, 2), (1, 1): (0, 3), (2, 1): (1, 3)}
    pump = [[8, 2, 3], [9, 4, 5, 0, 1], [6, 7, 2, 3, 8], [10, 11, 9, 0, 1, 4, 5]]
    for p in range(HEADS // 2):
        lanes = pair_lanes(p)
        for w in range(2):
            here = window(w)
            prob = probs[w * 4 + p]
            dmix = pair_stack(mixed[here, pl.ds(p * LANES, LANES)])
            query = pair_stack(qkv[here, lanes[0]])
            dprob = mm_nt(dmix, qkv[here, lanes[2]])
            dqkv[here, lanes[2]] = mm_tn(prob.astype(BF16), dmix).astype(BF16)
            dscore = prob * (dprob - jnp.sum(dprob * prob, axis=-1, keepdims=True)) * 0.125
            dscore = dscore.astype(BF16)
            dqkv[here, lanes[0]] = pair_join(mm(dscore, qkv[here, lanes[1]])).astype(BF16)
            dqkv[here, lanes[1]] = mm_tn(dscore, query).astype(BF16)
        if p % 2 == 1:
            for c in range(3):
                half, i = homes[c, p // 2]
                cut = pl.ds(c * width + (p // 2) * 256, 256)
                put(half, i, 0, mm_tn(h_a[...], dqkv[:, cut]).astype(BF16))
        step(*pump[p])

    dframe = None
    for c in range(3):
        part = pl.ds(c * width, width)
        term = mm_nt(dqkv[:, part], w_qkv[:, part])
        dframe = term if dframe is None else dframe + term
    dframe = dframe.astype(BF16).astype(F32)
    step(10, 11, 6, 7, 2, 3)
    term, gain_grad_a = norm_back(dframe, norm_a[...], jnp.concatenate(scale_a, axis=0), gain_a[...])
    for r in range(4):
        cut = slice(r * LANES, (r + 1) * LANES)
        gains_acc[0, r : r + 1, :] = gain_grad_a[:, cut]
        gains_acc[0, r + 4 : r + 5, :] = gain_grad_m[:, cut]
    gains_link = gain_chain()
    advance(gains_link)
    tok_f[...] = (resid[...] + term).astype(BF16)
    tok_lon = halo_go(tok_f, tok_right, grid["left"])
    level, row, col = row_cells()
    col, col_out = fold(col + per_level(level, cols), WW)
    back_pair = roll_pair(level * PLANE + row * WW + col, col_out, CELLS)
    sent_rows = pl.ds(0, CELLS - LEVELS * WW)

    def turn(arrived, own, other, rolled, rolled_x):
        arrived.wait_recv()
        rolled[...] = apply_roll(back_pair, own[...], other[...])
        rolled_x[pl.ds(CELLS - LEVELS * WW, LEVELS * WW), :] = jnp.zeros((LEVELS * WW, width), BF16)
        return halo_go(rolled.at[sent_rows], rolled_x.at[sent_rows], grid["above"])

    chains.append(gains_link)
    out_lat = turn(out_lon, out_f, out_right, out_t, out_tx)
    late = (9, 10, 11)
    step(4, 5, 6, 7, 8, 0, 1, 2, 3)
    step(*late, 12)
    step(4, 5, 6, 7, 0, 1, 2, 3, 8)
    step(*late, 12)
    tok_lat = turn(tok_lon, tok_f, tok_right, tok_t, tok_tx)
    step(*late, 12, 8)
    step(4, 5, 6, 7, *late, 12)
    step(0, 1, 2, 3, 8, *late)
    step(4, 5, 6, 7, 0, 1, 2, 3)
    step(8, *late, 4, 5, 6, 7)
    for again in range(9):
        step(*range(CHAINS + 1))
    for copy in (out_lat, tok_lat):
        copy.wait_recv()
    for copy in started:
        copy.wait_send()
    for copy in stores:
        copy.wait()


def finish_kernel(
    rows, cols, total_hbm, gains, out_t, out_tx, tok_t, tok_tx,
    block_out, grad_tokens, gain_a, gain_m, grad_qkv, grad_out, grad_up, grad_down,
    total, up, down, out, qkv, in_sems, out_sems,
):
    width = gain_a.shape[1]
    loads, moves = {}, []
    for i in range(CHAINS):
        for half in range(2):
            load = pltpu.make_async_copy(total_hbm.at[half, i], total.at[half, i], in_sems.at[half, i])
            load.start()
            loads[half, i] = load

    def put(half, i, j, stage, place):
        stage[place] = total[half, i, j * 512 : (j + 1) * 512, :].astype(F32)

    def move(src, dst):
        copy = pltpu.make_async_copy(src, dst, out_sems.at[len(moves)])
        copy.start()
        moves.append(copy)

    for c in range(CHUNKS):
        here = slice(c * 512, (c + 1) * 512)
        for half in range(2):
            for s in range(2):
                loads[half, 2 * c + s].wait()
                for j in range(2):
                    cut = slice((2 * s + j) * LANES, (2 * s + j + 1) * LANES)
                    if half == 0:
                        put(half, 2 * c + s, j, down, (here, cut))
                    else:
                        first = c * 512 + (2 * s + j) * LANES
                        put(half, 2 * c + s, j, up, (slice(None), slice(first, first + LANES)))
        move(down.at[pl.ds(c * 512, 512)], grad_down.at[pl.ds(c * 512, 512)])
        move(up.at[:, pl.ds(c * 512, 512)], grad_up.at[:, pl.ds(c * 512, 512)])
    homes = {(0, 1): (0, 0), (1, 1): (1, 0), (0, 2): (2, 0), (1, 2): (0, 1), (0, 3): (1, 1), (1, 3): (2, 1)}
    for i in range(4):
        for half in range(2):
            loads[half, 8 + i].wait()
            for j in range(2):
                if i == 0:
                    first = half * 256 + j * LANES
                    put(half, 8, j, out, (slice(None), slice(first, first + LANES)))
                else:
                    c, second = homes[half, i]
                    first = c * width + second * 256 + j * LANES
                    put(half, 8 + i, j, qkv, (slice(None), slice(first, first + LANES)))
        if i == 0:
            move(out, grad_out)
    move(qkv, grad_qkv)
    level, row, col = data_cells()
    row, row_out = fold(row + per_level(level, rows), WH)
    pair = roll_pair(row * LEVELS * WW + level * WW + col, row_out, CELLS)
    for own, other, result in ((out_t, out_tx, block_out), (tok_t, tok_tx, grad_tokens)):
        result[...] = apply_roll(pair, own[...], other[...]).reshape(result.shape)
    for r in range(4):
        cut = slice(r * LANES, (r + 1) * LANES)
        gain_a[:, cut] = gains[r : r + 1, :]
        gain_m[:, cut] = gains[r + 4 : r + 5, :]
    for copy in moves:
        copy.wait()


VMEM = pl.BlockSpec(memory_space=pltpu.VMEM)
SMEM = pl.BlockSpec(memory_space=pltpu.SMEM)
ANY = pl.BlockSpec(memory_space=pl.ANY)
DMA = pltpu.SemaphoreType.DMA


def call(kernel, outs, in_specs, out_specs, scratch, name, collective_id=None):
    params = {"vmem_limit_bytes": VMEM_BYTES}
    if collective_id is not None:
        params.update(collective_id=collective_id, has_side_effects=True)
    return pl.pallas_call(
        kernel,
        out_shape=[jax.ShapeDtypeStruct(shape, dtype) for shape, dtype in outs],
        in_specs=in_specs,
        out_specs=out_specs,
        scratch_shapes=scratch,
        compiler_params=pltpu.CompilerParams(**params),
        name=name,
    )


def sum_buffers():
    shapes = [(2, CHAINS, PART, LANES), (CHAINS, PART, LANES), (CHAINS, PART, LANES)]
    for r, count in enumerate(ROUNDS):
        shapes.append((CHAINS, SIDE - 1, count, LANES))
        if r < 2:
            shapes.append((CHAINS, count, LANES))
    shapes.append((2, CHAINS, PART, LANES))
    return [pltpu.VMEM(shape, BF16) for shape in shapes]


def native(field):
    return field.transpose(1, 2, 0, 3).reshape(-1, field.shape[0], field.shape[3])


def on_device(
    tokens,
    region_ids,
    shift_lat,
    shift_lon,
    gain_attn,
    w_qkv,
    w_out,
    gain_mlp,
    w_up,
    w_down,
    cotangent,
):
    levels, lat_rows, lon_cols, width = tokens.shape
    cells = levels * lat_rows * lon_cols
    ff = w_up.shape[1]
    lines = (lat_rows * lon_cols, levels, width)
    tile = ((cells, width), BF16)
    half, full = pltpu.VMEM((cells, width), BF16), pltpu.VMEM((cells, width), F32)
    total, gains_sum, out_t, out_tx, tok_t, tok_tx = call(
        block_kernel,
        [((2, CHAINS, PART, LANES), BF16), ((8, LANES), F32)] + [tile] * 4,
        [SMEM] * 2 + [VMEM] * 5 + [ANY] * 4,
        [ANY] + [VMEM] * 5,
        [pltpu.VMEM(w.shape, BF16) for w in (w_qkv, w_out, w_up, w_down)]
        + [pltpu.VMEM(lines, BF16)] * 2
        + [half] * 4
        + [pltpu.VMEM((16, LANES), jnp.int32)] * 2
        + [
            half,
            full,
            pltpu.VMEM((cells, LANES), BF16),
            full,
            half,
            pltpu.VMEM((cells, 3 * width), BF16),
            pltpu.VMEM((HEADS, 2 * WIN, WIN), F32),
            half,
            full,
            full,
            half,
            full,
            pltpu.VMEM((cells, 3 * width), BF16),
        ]
        + [half] * 4
        + [pltpu.VMEM((4, 8, LANES), F32), pltpu.VMEM((10, 8, LANES), F32)]
        + sum_buffers()
        + [
            DMA((4,)),
            DMA((12,)),
            DMA((12,)),
            DMA((CHAINS, SEMS)),
            DMA((CHAINS, SEMS)),
            DMA((10,)),
            DMA((10,)),
            DMA((2 * CHAINS,)),
        ],
        "block",
        0,
    )(
        shift_lat, shift_lon, native(tokens), native(cotangent), region_ids,
        gain_attn.reshape(1, width), gain_mlp.reshape(1, width), w_qkv, w_out, w_up, w_down,
    )
    results = call(
        finish_kernel,
        [
            (lines, BF16),
            (lines, BF16),
            ((1, width), F32),
            ((1, width), F32),
            ((width, 3 * width), F32),
            ((width, width), F32),
            ((width, ff), F32),
            ((ff, width), F32),
        ],
        [SMEM] * 2 + [ANY] + [VMEM] * 5,
        [VMEM] * 4 + [ANY] * 4,
        [
            pltpu.VMEM((2, CHAINS, PART, LANES), BF16),
            pltpu.VMEM(w_up.shape, F32),
            pltpu.VMEM(w_down.shape, F32),
            pltpu.VMEM(w_out.shape, F32),
            pltpu.VMEM(w_qkv.shape, F32),
            DMA((2, CHAINS)),
            DMA((2 * CHUNKS + 2,)),
        ],
        "finish",
    )(shift_lat, shift_lon, total, gains_sum, out_t, out_tx, tok_t, tok_tx)
    block_out, grad_tokens, grad_gain_attn, grad_gain_mlp, grad_qkv, grad_out, grad_up, grad_down = results

    def whole(field):
        return field.reshape(lat_rows, lon_cols, levels, width).transpose(2, 0, 1, 3)

    return (
        whole(block_out),
        whole(grad_tokens),
        grad_gain_attn.reshape(width),
        grad_qkv,
        grad_out,
        grad_gain_mlp.reshape(width),
        grad_up,
        grad_down,
    )


def solution(mesh):
    placed = (
        P(None, "lat", "lon", None),
        P("lat", "lon"),
        P(),
        P(),
        P(),
        P(),
        P(),
        P(),
        P(),
        P(),
        P(None, "lat", "lon", None),
    )
    return jax.shard_map(
        on_device,
        mesh=mesh,
        in_specs=placed,
        out_specs=(
            P(None, "lat", "lon", None),
            P(None, "lat", "lon", None),
            P(),
            P(),
            P(),
            P(),
            P(),
            P(),
        ),
        check_vma=False,
    )
```

time: 134 us -> 121 us (0.903)
  local copies, waits for them, and re-layouts: 7.44 us -> 0 us
  Pallas kernels: 126 us -> 120 us
    unnamed x4 -> x0, local copies, waits for them, and re-layouts: 7.44 us -> none
    pallas_call x1, Pallas kernels: 117 us -> 111 us  [on_device(): call(block_kernel, [((2, CHAINS, PART, LANES), BF16), ((8, LANES), F32)]...]
where the time goes in v3:
time: 121 us
  Pallas kernels  120 us (99%)
    pallas_call x1, Pallas kernels, on_device(): call(block_kernel, [((2, CHAINS, PART, LANES), BF16), ((8, LANES), F32)]...  111 us
    pallas_call x1, Pallas kernels, on_device(): call(finish_kernel, [(lines, BF16), (lines, BF16), ((1, width), F32), ((1...  9.19 us

profile of v3, /device:TPU:1, one launch (start us, length us, event | category | flops | bytes accessed | tf_op | source)
XLA Modules:
  0.0 121.1 jit_solution(8000458690608023403)
XLA Ops:
  0.6 111.1 %block.1 = (bf16[2,12,1024,128]{3,2,1,0:T(8,128)(2,1)}, f32[8,128]{1,0:T(8,128)}, bf16[288,512]{1,0:T(8,128)(2,1)}, bf16[288,512]{1,0:T(8,128)(2,1)}, bf16[288,5...) custom-call(s32[4]{0:T(128)} %rows.3, s32[4]{0:T(128)} %cols.3, bf16[72,4,512]{2,1,0:T(4,128)(2,1)} %bitcast.16, ...), custom_call_target="tpu_custom_call" | custom-call | tf_op jit(solution)/shard_map/block/pallas_call | solution.py:608
  111.8 9.2 %finish.1 = (bf16[72,4,512]{2,1,0:T(4,128)(2,1)}, bf16[72,4,512]{2,1,0:T(4,128)(2,1)}, f32[1,512]{1,0:T(1,128)}, f32[1,512]{1,0:T(1,128)}, f32[512,1536]{1,0:T(8...) custom-call(s32[4]{0:T(128)} %rows.3, s32[4]{0:T(128)} %cols.3, ...), custom_call_target="tpu_custom_call" | custom-call | tf_op jit(solution)/shard_map/finish/pallas_call | solution.py:651

commit v4 on v3

--- a/solution.py
+++ b/solution.py
@@ -22,10 +22,19 @@
 F32 = jnp.float32
 BF16 = jnp.bfloat16
 CHUNKS = 4
-CHAINS = 12
+FIRST_AXIS = (0, 1, 2, 1, 0, 2, 0, 1)
+GAINS, OUT, TOK = 8, 9, 10
+PUMP_MLP = ((), (), (0,), (1, 2))
+PUMP_PAIRS = ((3, 4), (5,), (), (6, 7, 5))
+PUMP_FRAME = (0, 6, 7, 1, 2)
+PUMP_TAIL = (
+    (5, OUT, 3, 1, 4, GAINS, 0, 7, 6, 3, 1, 2, 4, 7, GAINS, 0, 6, TOK, 3, 5, 7, 2, 1, 4, GAINS, 1, 6, 0)
+    + (GAINS, 5, 0, 4, 2, 3, 4, 2, 6, 5, 3, 7, 6, 5, 7)
+)
 PART = 1024
-ROUNDS = (256, 64, 16)
-SEMS = 20
+QUARTER = 256
+SHARE = 16
+ROUNDS = 6
 VMEM_BYTES = 60 * 1024 * 1024
 DIMS_ZERO = (((0,), (0,)), ((), ()))
 DIMS_LAST = (((1,), (1,)), ((), ()))
@@ -71,19 +80,22 @@
         x, y, z = lax.rem(x, SIDE), lax.rem(y, SIDE), lax.rem(z, SIDE)
         return ((y // 2) * 2 + core, z * 2 * SIDE + lax.rem(y, 2) * SIDE + x)
 
-    steps = range(1, SIDE)
-    peers = [
-        [device(x + j, y, z) for j in steps],
-        [device(x, y + j, z) for j in steps],
-        [device(x, y, z + j) for j in steps],
-    ]
+    spot = (x, y, z)
+
+    def away(offset):
+        return device(*[p + o for p, o in zip(spot, offset)])
+
+    offsets = [(i, j, k) for i in range(SIDE) for j in range(SIDE) for k in range(SIDE)]
+    peers = [[away([j * (a == b) for b in range(3)]) for j in range(1, SIDE)] for a in range(3)]
+    planes = [[(o, away(o)) for o in offsets if o[a] == 0 and any(o)] for a in range(3)]
+    known = [away(o) for o in offsets if 0 in o and any(o)]
     grid = {
         "below": (lax.rem(lat + 1, lats), lon),
         "above": (lax.rem(lat + lats - 1, lats), lon),
         "right": (lat, lax.rem(lon + 1, lons)),
         "left": (lat, lax.rem(lon + lons - 1, lons)),
     }
-    return grid, core, (y_hi * 2 + 1 - core, lon), peers, (x, y, z)
+    return grid, core, (y_hi * 2 + 1 - core, lon), peers, planes, known, spot
 
 
 def remote(src, dst, send, recv, device):
@@ -144,23 +156,24 @@
 
 def block_kernel(
     rows, cols, tok_in, cot_in, ids_in, gain_a, gain_m, w_qkv_hbm, w_out_hbm, w_up_hbm, w_down_hbm,
-    total_hbm, gains_sum, out_t, out_tx, tok_t, tok_tx,
+    total_a_hbm, total_b_hbm, gains_sum, out_t_hbm, out_tx_hbm, tok_t_hbm, tok_tx_hbm,
     w_qkv, w_out, w_up, w_down,
-    tok_above, cot_above, tok_rows, tok_left, cot_rows, cot_left, ids, ids_x,
+    tok_above, cot_left, tok_rows, tok_left, cot_cols, cot_above, ids, ids_x,
     cotf, tokf, labf, norm_a, h_a, qkv, probs, mixed, resid, norm_m, h_m, dh, dqkv,
-    out_f, out_right, tok_f, tok_right, gains_acc, gains_in,
-    partial, core_in, mine, r1, m1, r2, m2, r3, total,
+    out_f, out_right, tok_f, tok_right, out_t, out_tx, tok_t, tok_tx, gains_acc, gains_in,
+    part_a, core_a, mine_a, r1_a, m1_a, r2_a, total_a,
+    part_b, core_b, mine_b, r1_b, m1_b, r2_b, total_b,
     load_sem, halo_send, halo_recv, sum_send, sum_recv, gain_send, gain_recv, store_sem,
 ):
     width = gain_a.shape[1]
-    grid, core, core_peer, peers, position = places()
+    grid, core, core_peer, peers, planes, known, position = places()
     loads = [
         pltpu.make_async_copy(src, dst, load_sem.at[k])
         for k, (src, dst) in enumerate(
             ((w_qkv_hbm, w_qkv), (w_out_hbm, w_out), (w_up_hbm, w_up), (w_down_hbm, w_down))
         )
     ]
-    greeted = [core_peer] + [p for axis in peers for p in axis] + list(grid.values())
+    greeted = [core_peer] + known + list(grid.values())
     barrier = pltpu.get_barrier_semaphore()
     for device in greeted:
         pl.semaphore_signal(barrier, inc=1, device_id=device, device_id_type=MESH)
@@ -188,13 +201,21 @@
 
     ids[0:8, :] = jnp.zeros((8, LANES), jnp.int32)
     ids[0:WH, 0:WW] = ids_in[...]
-    for above in (tok_above, cot_above):
-        above[0:WW] = jnp.zeros((WW, LEVELS, width), BF16)
-    used_rows = pl.ds(WW, PLANE - WW)
+    tok_above[0:WW] = jnp.zeros((WW, LEVELS, width), BF16)
+    cot_left[:, 0:1] = jnp.zeros((WH, 1, LEVELS, width), BF16)
+    line = LEVELS * WW
+    cot_above[0:line, :] = jnp.zeros((line, width), BF16)
+    used_rows, used_cols, used_lines = pl.ds(WW, PLANE - WW), pl.ds(1, WW - 1), pl.ds(line, CELLS - line)
     pl.semaphore_wait(barrier, len(greeted))
     lat_tok = halo_go(tok_in.at[used_rows], tok_above.at[used_rows], grid["below"])
     lat_ids = halo_go(ids.at[pl.ds(0, 8)], ids.at[pl.ds(8, 8)], grid["below"])
-    lat_cot = halo_go(cot_in.at[used_rows], cot_above.at[used_rows], grid["below"])
+    lon_cot = halo_go(cot_in.at[:, used_cols], cot_left.at[:, used_cols], grid["right"])
+    level, row, col = row_cells()
+    col, col_out = fold(col - per_level(level, cols), WW)
+    first_pair = roll_pair((row * WW + col) * LEVELS + level, col_out, CELLS)
+    level, row, col = frame_cells(0, CELLS)
+    row, row_out = fold(row - per_level(level, rows), WH)
+    second_pair = roll_pair(row * line + level * WW + col, row_out, CELLS)
     level, row, col = frame_cells(0, CELLS)
     row, row_out = fold(row - per_level(level, rows), WH)
     row_pair = roll_pair((row * WW + col) * LEVELS + level, row_out, CELLS)
@@ -211,14 +232,11 @@
     lon_tok = [halo_go(tok_rows.at[window(w)], tok_left.at[window(w)], grid["right"]) for w in range(2)]
     lat_ids.wait_recv()
     lon_ids = halo_go(ids, ids_x, grid["right"])
-    lat_cot.wait_recv()
-    cot_rows[...] = apply_roll(
-        row_pair, cot_in[...].reshape(CELLS, width), cot_above[...].reshape(CELLS, width)
-    )
-    lon_cot = []
-
-    def lon_cot_go(w):
-        lon_cot.append(halo_go(cot_rows.at[window(w)], cot_left.at[window(w)], grid["right"]))
+    lon_cot.wait_recv()
+    cot_cols[...] = apply_roll(
+        first_pair, cot_in[...].reshape(CELLS, width), cot_left[...].reshape(CELLS, width)
+    )
+    lat_cot = halo_go(cot_cols.at[used_lines], cot_above.at[used_lines], grid["below"])
 
     lon_ids.wait_recv()
     ids_all = jnp.concatenate([ids[...], ids_x[...]], axis=0).astype(F32).astype(BF16)
@@ -234,7 +252,6 @@
     def forward_in(w):
         here = window(w)
         lon_tok[w].wait_recv()
-        lon_cot_go(w)
         values = apply_roll(col_pairs[w], tok_rows[here, :], tok_left[here, :]).astype(F32)
         tokf[here, :] = values
         normed, scale = norm_stats(values)
@@ -284,11 +301,12 @@
     norm_m[...] = normed
     h_m[...] = (normed * gain_m[...]).astype(BF16)
     dh[...] = jnp.zeros_like(dh)
-    for w in range(2):
-        lon_cot[w].wait_recv()
-        cotf[window(w), :] = apply_roll(col_pairs[w], cot_rows[window(w), :], cot_left[window(w), :])
-
-    arrivals, sums = (r1, r2, r3), (mine, m1, m2)
+    lat_cot.wait_recv()
+    cotf[...] = apply_roll(second_pair, cot_cols[...], cot_above[...])
+
+    set_a = (part_a, core_a, mine_a, r1_a, m1_a, r2_a, total_a, total_a_hbm)
+    set_b = (part_b, core_b, mine_b, r1_b, m1_b, r2_b, total_b, total_b_hbm)
+    sent = []
 
     def block(offset, count):
         return pl.ds(pl.multiple_of(offset, 16), count)
@@ -298,52 +316,59 @@
         copy.start()
         stores.append(copy)
 
-    def chain(i):
-        order = [(i + r) % 3 for r in range(3)]
-        used = [0]
-
-        def send(src, dst, device):
-            n = used[0]
-            used[0] += 1
-            return go(src, dst, sum_send.at[i, n], sum_recv.at[i, n], device)
-
-        first = send(partial.at[1 - core, i], core_in.at[i], core_peer)
-        yield
-        first.wait_recv()
+    def chain(refs, i, k):
+        partial, core_in, mine, r1, m1, r2, total, total_hbm = refs
+        axis = FIRST_AXIS[k]
+        plane = planes[axis]
+        at = position[axis]
+        rest = [a for a in range(3) if a != axis]
+
+        def share(offset):
+            first, second = [lax.rem(position[a] + offset[a], SIDE) for a in rest]
+            return (first * SIDE + second) * SHARE
+
+        def send(n, src, dst, device):
+            remote(src, dst, sum_send.at[k, n], sum_recv.at[k, n], device).start()
+
+        def arrive(n, like):
+            whole = remote(like, like, sum_send.at[k, n], sum_recv.at[k, n], core_peer)
+            sent.append(whole)
+            whole.wait_recv()
+
+        send(0, partial.at[1 - core, i], core_in.at[i], core_peer)
+        yield
+        arrive(0, core_in.at[i])
         mine[i] = (partial[core, i].astype(F32) + core_in[i].astype(F32)).astype(BF16)
-        offset, offsets = 0, []
-        for r, count in enumerate(ROUNDS):
-            at = position[order[r]]
-            copies = [
-                send(
-                    sums[r].at[i, block(lax.rem(at + j, SIDE) * count, count)],
-                    arrivals[r].at[i, j - 1],
-                    peers[order[r]][j - 1],
-                )
-                for j in range(1, SIDE)
-            ]
-            yield
-            for copy in copies:
-                copy.wait_recv()
-            summed = sums[r][i, block(at * count, count), :].astype(F32)
-            for j in range(SIDE - 1):
-                summed = summed + arrivals[r][i, j].astype(F32)
-            offset = offset + at * count
-            offsets.append(offset)
-            if r < 2:
-                sums[r + 1][i] = summed.astype(BF16)
-            else:
-                total[core, i, block(offset, count), :] = summed.astype(BF16)
-        for r in reversed(range(3)):
-            place = total.at[core, i, block(offsets[r], ROUNDS[r])]
-            copies = [send(place, place, peers[order[r]][j]) for j in range(SIDE - 1)]
-            yield
-            for copy in copies:
-                copy.wait_recv()
-        last = send(total.at[core, i], total.at[core, i], core_peer)
+        for j in range(1, SIDE):
+            quarter = block(lax.rem(at + j, SIDE) * QUARTER, QUARTER)
+            send(1, mine.at[i, quarter], r1.at[i, j - 1], peers[axis][j - 1])
+        yield
+        arrive(1, r1.at[i])
+        summed = mine[i, block(at * QUARTER, QUARTER), :].astype(F32)
+        for j in range(SIDE - 1):
+            summed = summed + r1[i, j].astype(F32)
+        m1[i] = summed.astype(BF16)
+        for n, (offset, device) in enumerate(plane):
+            send(2, m1.at[i, block(share(offset), SHARE)], r2.at[i, n], device)
+        yield
+        arrive(2, r2.at[i])
+        own = share((0, 0, 0))
+        summed = m1[i, block(own, SHARE), :].astype(F32) + jnp.sum(r2[i].astype(F32), axis=0)
+        place = (core, i, block(at * QUARTER + own, SHARE))
+        total[place] = summed.astype(BF16)
+        for offset, device in plane:
+            send(3, total.at[place], total.at[place], device)
+        yield
+        arrive(3, r2.at[i])
+        place = (core, i, block(at * QUARTER, QUARTER))
+        for device in peers[axis]:
+            send(4, total.at[place], total.at[place], device)
+        yield
+        arrive(4, r1.at[i])
+        send(5, total.at[core, i], total.at[core, i], core_peer)
         store(total.at[core, i], total_hbm.at[core, i])
         yield
-        last.wait_recv()
+        arrive(5, core_in.at[i])
         store(total.at[1 - core, i], total_hbm.at[1 - core, i])
 
     def gain_chain():
@@ -374,7 +399,8 @@
         for link in chains:
             next(link, None)
 
-    chains = [chain(i) for i in range(CHAINS)]
+    chains = [chain(set_a, i, i) for i in range(CHUNKS)]
+    chains += [chain(set_b, i, CHUNKS + i) for i in range(CHUNKS)]
 
     def step(*which):
         for i in which:
@@ -391,14 +417,12 @@
         dh[...] += mm_nt(grad_pre, w_up[:, part])
         down = mm_tn(act, cotf[...]).astype(BF16)
         up = mm_tn(h_m[...], grad_pre).astype(BF16)
-        for b in range(4):
-            spot = slice((b % 2) * 512, (b % 2 + 1) * 512)
-            cut = slice(b * LANES, (b + 1) * LANES)
-            partial[0, 2 * c + b // 2, spot, :] = down[:, cut]
-            partial[1, 2 * c + b // 2, spot, :] = up[:, cut]
-        step(2 * c, 2 * c + 1)
-        if c > 0:
-            step(2 * c - 2, 2 * c - 1)
+        for b in range(2):
+            spot = slice(b * 512, (b + 1) * 512)
+            cut = slice(b * 256, (b + 1) * 256)
+            part_a[0, c, spot, :] = down[:, cut]
+            part_a[1, c, spot, :] = up[:, cut]
+        step(c, *PUMP_MLP[c])
     out_f[...] = resid[...].astype(BF16)
     out_lon = halo_go(out_f, out_right, grid["left"])
     term, gain_grad_m = norm_back(dh[...], norm_m[...], scale_m, gain_m[...])
@@ -407,17 +431,15 @@
 
     def put(half, i, b, value):
         for j in range(2):
-            partial[half, 8 + i, j * 512 : (j + 1) * 512, :] = value[:, b + j * LANES : b + (j + 1) * LANES]
+            part_b[half, i, j * 512 : (j + 1) * 512, :] = value[:, b + j * LANES : b + (j + 1) * LANES]
 
     grad_out = mm_tn(mixed[...], grad_attn).astype(BF16)
     put(0, 0, 0, grad_out)
     put(1, 0, 256, grad_out)
-    step(8, 6, 7)
+    step(4)
     mixed[...] = mm_nt(grad_attn, w_out[...]).astype(BF16)
-    step(0, 1)
 
     homes = {(0, 0): (0, 1), (1, 0): (1, 1), (2, 0): (0, 2), (0, 1): (1, 2), (1, 1): (0, 3), (2, 1): (1, 3)}
-    pump = [[8, 2, 3], [9, 4, 5, 0, 1], [6, 7, 2, 3, 8], [10, 11, 9, 0, 1, 4, 5]]
     for p in range(HEADS // 2):
         lanes = pair_lanes(p)
         for w in range(2):
@@ -436,7 +458,7 @@
                 half, i = homes[c, p // 2]
                 cut = pl.ds(c * width + (p // 2) * 256, 256)
                 put(half, i, 0, mm_tn(h_a[...], dqkv[:, cut]).astype(BF16))
-        step(*pump[p])
+        step(*PUMP_PAIRS[p])
 
     dframe = None
     for c in range(3):
@@ -444,7 +466,7 @@
         term = mm_nt(dqkv[:, part], w_qkv[:, part])
         dframe = term if dframe is None else dframe + term
     dframe = dframe.astype(BF16).astype(F32)
-    step(10, 11, 6, 7, 2, 3)
+    step(*PUMP_FRAME)
     term, gain_grad_a = norm_back(dframe, norm_a[...], jnp.concatenate(scale_a, axis=0), gain_a[...])
     for r in range(4):
         cut = slice(r * LANES, (r + 1) * LANES)
@@ -459,29 +481,33 @@
     back_pair = roll_pair(level * PLANE + row * WW + col, col_out, CELLS)
     sent_rows = pl.ds(0, CELLS - LEVELS * WW)
 
-    def turn(arrived, own, other, rolled, rolled_x):
+    def turn(arrived, own, other, rolled, rolled_x, rolled_hbm):
         arrived.wait_recv()
         rolled[...] = apply_roll(back_pair, own[...], other[...])
         rolled_x[pl.ds(CELLS - LEVELS * WW, LEVELS * WW), :] = jnp.zeros((LEVELS * WW, width), BF16)
+        store(rolled, rolled_hbm)
         return halo_go(rolled.at[sent_rows], rolled_x.at[sent_rows], grid["above"])
 
     chains.append(gains_link)
-    out_lat = turn(out_lon, out_f, out_right, out_t, out_tx)
-    late = (9, 10, 11)
-    step(4, 5, 6, 7, 8, 0, 1, 2, 3)
-    step(*late, 12)
-    step(4, 5, 6, 7, 0, 1, 2, 3, 8)
-    step(*late, 12)
-    tok_lat = turn(tok_lon, tok_f, tok_right, tok_t, tok_tx)
-    step(*late, 12, 8)
-    step(4, 5, 6, 7, *late, 12)
-    step(0, 1, 2, 3, 8, *late)
-    step(4, 5, 6, 7, 0, 1, 2, 3)
-    step(8, *late, 4, 5, 6, 7)
-    for again in range(9):
-        step(*range(CHAINS + 1))
-    for copy in (out_lat, tok_lat):
+    lat_back = []
+
+    def out_back():
+        lat_back.append(turn(out_lon, out_f, out_right, out_t, out_tx, out_t_hbm))
+        yield
+
+    def tok_back():
+        lat_back.append(turn(tok_lon, tok_f, tok_right, tok_t, tok_tx, tok_t_hbm))
+        yield
+
+    chains.extend((out_back(), tok_back()))
+    step(*PUMP_TAIL)
+    for again in range(ROUNDS):
+        step(*range(CHUNKS * 2 + 1))
+    for copy, rolled_x, rolled_hbm in zip(lat_back, (out_tx, tok_tx), (out_tx_hbm, tok_tx_hbm)):
         copy.wait_recv()
+        store(rolled_x, rolled_hbm)
+    for copy in sent:
+        copy.wait_send()
     for copy in started:
         copy.wait_send()
     for copy in stores:
@@ -489,60 +515,65 @@
 
 
 def finish_kernel(
-    rows, cols, total_hbm, gains, out_t, out_tx, tok_t, tok_tx,
+    rows, cols, total_a_hbm, total_b_hbm, gains, out_t_hbm, out_tx_hbm, tok_t_hbm, tok_tx_hbm,
     block_out, grad_tokens, gain_a, gain_m, grad_qkv, grad_out, grad_up, grad_down,
-    total, up, down, out, qkv, in_sems, out_sems,
+    total_a, total_b, up, down, out, qkv, tiles, results, in_sems, tile_sems, out_sems,
 ):
     width = gain_a.shape[1]
     loads, moves = {}, []
-    for i in range(CHAINS):
-        for half in range(2):
-            load = pltpu.make_async_copy(total_hbm.at[half, i], total.at[half, i], in_sems.at[half, i])
-            load.start()
-            loads[half, i] = load
-
-    def put(half, i, j, stage, place):
-        stage[place] = total[half, i, j * 512 : (j + 1) * 512, :].astype(F32)
+    for i in range(CHUNKS):
+        for kind, (src, dst) in enumerate(((total_a_hbm, total_a), (total_b_hbm, total_b))):
+            for half in range(2):
+                load = pltpu.make_async_copy(src.at[half, i], dst.at[half, i], in_sems.at[kind, half, i])
+                load.start()
+                loads[kind, half, i] = load
+    tile_loads = [
+        pltpu.make_async_copy(src, tiles.at[n], tile_sems.at[n])
+        for n, src in enumerate((out_t_hbm, out_tx_hbm, tok_t_hbm, tok_tx_hbm))
+    ]
+    for load in tile_loads:
+        load.start()
 
     def move(src, dst):
         copy = pltpu.make_async_copy(src, dst, out_sems.at[len(moves)])
         copy.start()
         moves.append(copy)
 
-    for c in range(CHUNKS):
-        here = slice(c * 512, (c + 1) * 512)
+    homes = {(0, 1): (0, 0), (1, 1): (1, 0), (0, 2): (2, 0), (1, 2): (0, 1), (0, 3): (1, 1), (1, 3): (2, 1)}
+    for i in range(CHUNKS):
+        here = slice(i * 512, (i + 1) * 512)
         for half in range(2):
-            for s in range(2):
-                loads[half, 2 * c + s].wait()
-                for j in range(2):
-                    cut = slice((2 * s + j) * LANES, (2 * s + j + 1) * LANES)
-                    if half == 0:
-                        put(half, 2 * c + s, j, down, (here, cut))
-                    else:
-                        first = c * 512 + (2 * s + j) * LANES
-                        put(half, 2 * c + s, j, up, (slice(None), slice(first, first + LANES)))
-        move(down.at[pl.ds(c * 512, 512)], grad_down.at[pl.ds(c * 512, 512)])
-        move(up.at[:, pl.ds(c * 512, 512)], grad_up.at[:, pl.ds(c * 512, 512)])
-    homes = {(0, 1): (0, 0), (1, 1): (1, 0), (0, 2): (2, 0), (1, 2): (0, 1), (0, 3): (1, 1), (1, 3): (2, 1)}
-    for i in range(4):
+            loads[0, half, i].wait()
+            for b in range(2):
+                value = total_a[half, i, b * 512 : (b + 1) * 512, :].astype(F32)
+                if half == 0:
+                    down[here, b * 256 : (b + 1) * 256] = value
+                else:
+                    up[:, i * 512 + b * 256 : i * 512 + (b + 1) * 256] = value
+        move(down.at[pl.ds(i * 512, 512)], grad_down.at[pl.ds(i * 512, 512)])
+        move(up.at[:, pl.ds(i * 512, 512)], grad_up.at[:, pl.ds(i * 512, 512)])
         for half in range(2):
-            loads[half, 8 + i].wait()
+            loads[1, half, i].wait()
             for j in range(2):
+                value = total_b[half, i, j * 512 : (j + 1) * 512, :].astype(F32)
                 if i == 0:
                     first = half * 256 + j * LANES
-                    put(half, 8, j, out, (slice(None), slice(first, first + LANES)))
+                    out[:, first : first + LANES] = value
                 else:
                     c, second = homes[half, i]
                     first = c * width + second * 256 + j * LANES
-                    put(half, 8 + i, j, qkv, (slice(None), slice(first, first + LANES)))
+                    qkv[:, first : first + LANES] = value
         if i == 0:
             move(out, grad_out)
     move(qkv, grad_qkv)
     level, row, col = data_cells()
     row, row_out = fold(row + per_level(level, rows), WH)
     pair = roll_pair(row * LEVELS * WW + level * WW + col, row_out, CELLS)
-    for own, other, result in ((out_t, out_tx, block_out), (tok_t, tok_tx, grad_tokens)):
-        result[...] = apply_roll(pair, own[...], other[...]).reshape(result.shape)
+    for load in tile_loads:
+        load.wait()
+    for n, result in enumerate((block_out, grad_tokens)):
+        results[n] = apply_roll(pair, tiles[2 * n], tiles[2 * n + 1]).reshape(result.shape)
+        move(results.at[n], result)
     for r in range(4):
         cut = slice(r * LANES, (r + 1) * LANES)
         gain_a[:, cut] = gains[r : r + 1, :]
@@ -572,13 +603,16 @@
     )
 
 
-def sum_buffers():
-    shapes = [(2, CHAINS, PART, LANES), (CHAINS, PART, LANES), (CHAINS, PART, LANES)]
-    for r, count in enumerate(ROUNDS):
-        shapes.append((CHAINS, SIDE - 1, count, LANES))
-        if r < 2:
-            shapes.append((CHAINS, count, LANES))
-    shapes.append((2, CHAINS, PART, LANES))
+def sum_buffers(lanes):
+    shapes = [
+        (2, CHUNKS, PART, lanes),
+        (CHUNKS, PART, lanes),
+        (CHUNKS, PART, lanes),
+        (CHUNKS, SIDE - 1, QUARTER, lanes),
+        (CHUNKS, QUARTER, lanes),
+        (CHUNKS, SIDE * SIDE - 1, SHARE, lanes),
+        (2, CHUNKS, PART, lanes),
+    ]
     return [pltpu.VMEM(shape, BF16) for shape in shapes]
 
 
@@ -605,13 +639,13 @@
     lines = (lat_rows * lon_cols, levels, width)
     tile = ((cells, width), BF16)
     half, full = pltpu.VMEM((cells, width), BF16), pltpu.VMEM((cells, width), F32)
-    total, gains_sum, out_t, out_tx, tok_t, tok_tx = call(
+    total_a, total_b, gains_sum, *rolled = call(
         block_kernel,
-        [((2, CHAINS, PART, LANES), BF16), ((8, LANES), F32)] + [tile] * 4,
+        [((2, CHUNKS, PART, 256), BF16), ((2, CHUNKS, PART, LANES), BF16), ((8, LANES), F32)] + [tile] * 4,
         [SMEM] * 2 + [VMEM] * 5 + [ANY] * 4,
-        [ANY] + [VMEM] * 5,
+        [ANY] * 2 + [VMEM] + [ANY] * 4,
         [pltpu.VMEM(w.shape, BF16) for w in (w_qkv, w_out, w_up, w_down)]
-        + [pltpu.VMEM(lines, BF16)] * 2
+        + [pltpu.VMEM(lines, BF16), pltpu.VMEM((lat_rows, lon_cols, levels, width), BF16)]
         + [half] * 4
         + [pltpu.VMEM((16, LANES), jnp.int32)] * 2
         + [
@@ -629,23 +663,24 @@
             full,
             pltpu.VMEM((cells, 3 * width), BF16),
         ]
-        + [half] * 4
+        + [half] * 8
         + [pltpu.VMEM((4, 8, LANES), F32), pltpu.VMEM((10, 8, LANES), F32)]
-        + sum_buffers()
+        + sum_buffers(256)
+        + sum_buffers(LANES)
         + [
             DMA((4,)),
-            DMA((12,)),
-            DMA((12,)),
-            DMA((CHAINS, SEMS)),
-            DMA((CHAINS, SEMS)),
+            DMA((11,)),
+            DMA((11,)),
+            DMA((2 * CHUNKS, ROUNDS)),
+            DMA((2 * CHUNKS, ROUNDS)),
             DMA((10,)),
             DMA((10,)),
-            DMA((2 * CHAINS,)),
+            DMA((4 * CHUNKS + 4,)),
         ],
         "block",
         0,
     )(
-        shift_lat, shift_lon, native(tokens), native(cotangent), region_ids,
+        shift_lat, shift_lon, native(tokens), cotangent.transpose(1, 2, 0, 3), region_ids,
         gain_attn.reshape(1, width), gain_mlp.reshape(1, width), w_qkv, w_out, w_up, w_down,
     )
     results = call(
@@ -660,19 +695,23 @@
             ((width, ff), F32),
             ((ff, width), F32),
         ],
-        [SMEM] * 2 + [ANY] + [VMEM] * 5,
-        [VMEM] * 4 + [ANY] * 4,
+        [SMEM] * 2 + [ANY] * 2 + [VMEM] + [ANY] * 4,
+        [ANY] * 2 + [VMEM] * 2 + [ANY] * 4,
         [
-            pltpu.VMEM((2, CHAINS, PART, LANES), BF16),
+            pltpu.VMEM((2, CHUNKS, PART, 256), BF16),
+            pltpu.VMEM((2, CHUNKS, PART, LANES), BF16),
             pltpu.VMEM(w_up.shape, F32),
             pltpu.VMEM(w_down.shape, F32),
             pltpu.VMEM(w_out.shape, F32),
             pltpu.VMEM(w_qkv.shape, F32),
-            DMA((2, CHAINS)),
-            DMA((2 * CHUNKS + 2,)),
+            pltpu.VMEM((4, cells, width), BF16),
+            pltpu.VMEM((2,) + lines, BF16),
+            DMA((2, 2, CHUNKS)),
+            DMA((4,)),
+            DMA((2 * CHUNKS + 4,)),
         ],
         "finish",
-    )(shift_lat, shift_lon, total, gains_sum, out_t, out_tx, tok_t, tok_tx)
+    )(shift_lat, shift_lon, total_a, total_b, gains_sum, *rolled)
     block_out, grad_tokens, grad_gain_attn, grad_gain_mlp, grad_qkv, grad_out, grad_up, grad_down = results
 
     def whole(field):

time: 121 us -> 114 us (0.942)
  Pallas kernels: 120 us -> 113 us
    pallas_call x1, Pallas kernels: 111 us -> 104 us  [on_device(): call(block_kernel, [((2, CHUNKS, PART, 256), BF16), ((2, CHUNKS, PART, LA...]
where the time goes in v4:
time: 114 us
  Pallas kernels  113 us (99%)
    pallas_call x1, Pallas kernels, on_device(): call(block_kernel, [((2, CHUNKS, PART, 256), BF16), ((2, CHUNKS, PART, LA...  104 us
    pallas_call x1, Pallas kernels, on_device(): call(finish_kernel, [(lines, BF16), (lines, BF16), ((1, width), F32), ((1...  9.09 us

profile of v4, /device:TPU:1, one launch (start us, length us, event | category | flops | bytes accessed | tf_op | source)
XLA Modules:
  0.0 114.2 jit_solution(7579229221726792627)
XLA Ops:
  0.6 104.3 %block.1 = (bf16[2,4,1024,256]{3,2,1,0:T(8,128)(2,1)}, bf16[2,4,1024,128]{3,2,1,0:T(8,128)(2,1)}, f32[8,128]{1,0:T(8,128)}, bf16[288,512]{1,0:T(8,128)(2,1)}, bf...) custom-call(s32[4]{0:T(128)} %rows.3, s32[4]{0:T(128)} %cols.3, ...), custom_call_target="tpu_custom_call" | custom-call | tf_op jit(solution)/shard_map/block/pallas_call | solution.py:642
  104.9 9.1 %finish.1 = (bf16[72,4,512]{2,1,0:T(4,128)(2,1)}, bf16[72,4,512]{2,1,0:T(4,128)(2,1)}, f32[1,512]{1,0:T(1,128)}, f32[1,512]{1,0:T(1,128)}, f32[512,1536]{1,0:T(8...) custom-call(s32[4]{0:T(128)} %rows.3, s32[4]{0:T(128)} %cols.3, ...), custom_call_target="tpu_custom_call" | custom-call | tf_op jit(solution)/shard_map/finish/pallas_call | solution.py:686

commit v5 on v4

--- a/solution.py
+++ b/solution.py
@@ -22,15 +22,13 @@
 F32 = jnp.float32
 BF16 = jnp.bfloat16
 CHUNKS = 4
-FIRST_AXIS = (0, 1, 2, 1, 0, 2, 0, 1)
+FIRST_AXIS = (1, 2, 1, 0, 2, 1, 2, 2)
 GAINS, OUT, TOK = 8, 9, 10
-PUMP_MLP = ((), (), (0,), (1, 2))
-PUMP_PAIRS = ((3, 4), (5,), (), (6, 7, 5))
-PUMP_FRAME = (0, 6, 7, 1, 2)
-PUMP_TAIL = (
-    (5, OUT, 3, 1, 4, GAINS, 0, 7, 6, 3, 1, 2, 4, 7, GAINS, 0, 6, TOK, 3, 5, 7, 2, 1, 4, GAINS, 1, 6, 0)
-    + (GAINS, 5, 0, 4, 2, 3, 4, 2, 6, 5, 3, 7, 6, 5, 7)
-)
+PUMP_MLP = ((0,), (1,), (2, 0), (3, 1, 2))
+PUMP_OUT, PUMP_MIX = (4, 3), ()
+PUMP_PAIRS = ((4,), (5,), (), (6, 7, 5, 0, 9, 6, 7, 1))
+PUMP_FRAME = ()
+PUMP_TAIL = (4, 8, 2, 3, 0, 5, 6, 1, 7, 10, 8, 3, 2, 4, 0, 6, 5, 1, 8, 7, 2, 4, 3, 6, 5, 7, 0, 8, 1, 0, 1, 4, 3, 2, 4, 6, 3, 5, 2, 6, 7, 5, 7)
 PART = 1024
 QUARTER = 256
 SHARE = 16
@@ -196,6 +194,15 @@
         halos.append(go(src, dst, halo_send.at[k], halo_recv.at[k], device))
         return halos[-1]
 
+    def halo_split(src, dst, device, start, count, pieces):
+        size = count // pieces
+        cuts = [pl.ds(start + n * size, size) for n in range(pieces)]
+        return [halo_go(src.at[cut], dst.at[cut], device) for cut in cuts]
+
+    def arrived(copies):
+        for copy in copies:
+            copy.wait_recv()
+
     def window(w):
         return pl.ds(w * WIN, WIN)
 
@@ -205,9 +212,9 @@
     cot_left[:, 0:1] = jnp.zeros((WH, 1, LEVELS, width), BF16)
     line = LEVELS * WW
     cot_above[0:line, :] = jnp.zeros((line, width), BF16)
-    used_rows, used_cols, used_lines = pl.ds(WW, PLANE - WW), pl.ds(1, WW - 1), pl.ds(line, CELLS - line)
+    used_cols = pl.ds(1, WW - 1)
     pl.semaphore_wait(barrier, len(greeted))
-    lat_tok = halo_go(tok_in.at[used_rows], tok_above.at[used_rows], grid["below"])
+    lat_tok = halo_split(tok_in, tok_above, grid["below"], WW, PLANE - WW, 4)
     lat_ids = halo_go(ids.at[pl.ds(0, 8)], ids.at[pl.ds(8, 8)], grid["below"])
     lon_cot = halo_go(cot_in.at[:, used_cols], cot_left.at[:, used_cols], grid["right"])
     level, row, col = row_cells()
@@ -225,7 +232,7 @@
     col_pairs = [
         roll_pair(col_index[w * WIN : (w + 1) * WIN], col_out[w * WIN : (w + 1) * WIN], WIN) for w in range(2)
     ]
-    lat_tok.wait_recv()
+    arrived(lat_tok)
     tok_rows[...] = apply_roll(
         row_pair, tok_in[...].reshape(CELLS, width), tok_above[...].reshape(CELLS, width)
     )
@@ -236,7 +243,7 @@
     cot_cols[...] = apply_roll(
         first_pair, cot_in[...].reshape(CELLS, width), cot_left[...].reshape(CELLS, width)
     )
-    lat_cot = halo_go(cot_cols.at[used_lines], cot_above.at[used_lines], grid["below"])
+    lat_cot = halo_split(cot_cols, cot_above, grid["below"], line, CELLS - line, 3)
 
     lon_ids.wait_recv()
     ids_all = jnp.concatenate([ids[...], ids_x[...]], axis=0).astype(F32).astype(BF16)
@@ -301,7 +308,7 @@
     norm_m[...] = normed
     h_m[...] = (normed * gain_m[...]).astype(BF16)
     dh[...] = jnp.zeros_like(dh)
-    lat_cot.wait_recv()
+    arrived(lat_cot)
     cotf[...] = apply_roll(second_pair, cot_cols[...], cot_above[...])
 
     set_a = (part_a, core_a, mine_a, r1_a, m1_a, r2_a, total_a, total_a_hbm)
@@ -406,6 +413,30 @@
         for i in which:
             next(chains[i], None)
 
+    level, row, col = row_cells()
+    col, col_out = fold(col + per_level(level, cols), WW)
+    back_pair = roll_pair(level * PLANE + row * WW + col, col_out, CELLS)
+
+    def turn(arrived, own, other, rolled, rolled_x, rolled_hbm):
+        arrived.wait_recv()
+        rolled[...] = apply_roll(back_pair, own[...], other[...])
+        rolled_x[pl.ds(CELLS - LEVELS * WW, LEVELS * WW), :] = jnp.zeros((LEVELS * WW, width), BF16)
+        store(rolled, rolled_hbm)
+        return halo_split(rolled, rolled_x, grid["above"], 0, CELLS - line, 3)
+
+    gains_link = gain_chain()
+    chains.append(gains_link)
+    lat_back, halo_lon = [], []
+
+    def out_back():
+        lat_back.append(turn(halo_lon[0], out_f, out_right, out_t, out_tx, out_t_hbm))
+        yield
+
+    def tok_back():
+        lat_back.append(turn(halo_lon[1], tok_f, tok_right, tok_t, tok_tx, tok_t_hbm))
+        yield
+
+    chains.extend((out_back(), tok_back()))
     for c in range(CHUNKS):
         part = pl.ds(c * 512, 512)
         pre = mm(h_m[...], w_up[:, part])
@@ -422,9 +453,9 @@
             cut = slice(b * 256, (b + 1) * 256)
             part_a[0, c, spot, :] = down[:, cut]
             part_a[1, c, spot, :] = up[:, cut]
-        step(c, *PUMP_MLP[c])
+        step(*PUMP_MLP[c])
     out_f[...] = resid[...].astype(BF16)
-    out_lon = halo_go(out_f, out_right, grid["left"])
+    halo_lon.append(halo_go(out_f, out_right, grid["left"]))
     term, gain_grad_m = norm_back(dh[...], norm_m[...], scale_m, gain_m[...])
     resid[...] = cotf[...].astype(F32) + term
     grad_attn = resid[...].astype(BF16)
@@ -436,8 +467,9 @@
     grad_out = mm_tn(mixed[...], grad_attn).astype(BF16)
     put(0, 0, 0, grad_out)
     put(1, 0, 256, grad_out)
-    step(4)
+    step(*PUMP_OUT)
     mixed[...] = mm_nt(grad_attn, w_out[...]).astype(BF16)
+    step(*PUMP_MIX)
 
     homes = {(0, 0): (0, 1), (1, 0): (1, 1), (2, 0): (0, 2), (0, 1): (1, 2), (1, 1): (0, 3), (2, 1): (1, 3)}
     for p in range(HEADS // 2):
@@ -472,39 +504,14 @@
         cut = slice(r * LANES, (r + 1) * LANES)
         gains_acc[0, r : r + 1, :] = gain_grad_a[:, cut]
         gains_acc[0, r + 4 : r + 5, :] = gain_grad_m[:, cut]
-    gains_link = gain_chain()
     advance(gains_link)
     tok_f[...] = (resid[...] + term).astype(BF16)
-    tok_lon = halo_go(tok_f, tok_right, grid["left"])
-    level, row, col = row_cells()
-    col, col_out = fold(col + per_level(level, cols), WW)
-    back_pair = roll_pair(level * PLANE + row * WW + col, col_out, CELLS)
-    sent_rows = pl.ds(0, CELLS - LEVELS * WW)
-
-    def turn(arrived, own, other, rolled, rolled_x, rolled_hbm):
-        arrived.wait_recv()
-        rolled[...] = apply_roll(back_pair, own[...], other[...])
-        rolled_x[pl.ds(CELLS - LEVELS * WW, LEVELS * WW), :] = jnp.zeros((LEVELS * WW, width), BF16)
-        store(rolled, rolled_hbm)
-        return halo_go(rolled.at[sent_rows], rolled_x.at[sent_rows], grid["above"])
-
-    chains.append(gains_link)
-    lat_back = []
-
-    def out_back():
-        lat_back.append(turn(out_lon, out_f, out_right, out_t, out_tx, out_t_hbm))
-        yield
-
-    def tok_back():
-        lat_back.append(turn(tok_lon, tok_f, tok_right, tok_t, tok_tx, tok_t_hbm))
-        yield
-
-    chains.extend((out_back(), tok_back()))
+    halo_lon.append(halo_go(tok_f, tok_right, grid["left"]))
     step(*PUMP_TAIL)
     for again in range(ROUNDS):
         step(*range(CHUNKS * 2 + 1))
     for copy, rolled_x, rolled_hbm in zip(lat_back, (out_tx, tok_tx), (out_tx_hbm, tok_tx_hbm)):
-        copy.wait_recv()
+        arrived(copy)
         store(rolled_x, rolled_hbm)
     for copy in sent:
         copy.wait_send()
@@ -669,8 +676,8 @@
         + sum_buffers(LANES)
         + [
             DMA((4,)),
-            DMA((11,)),
-            DMA((11,)),
+            DMA((20,)),
+            DMA((20,)),
             DMA((2 * CHUNKS, ROUNDS)),
             DMA((2 * CHUNKS, ROUNDS)),
             DMA((10,)),

time: 114 us -> 108 us (0.947)
  Pallas kernels: 113 us -> 107 us
    pallas_call x1, Pallas kernels: 104 us -> 97.8 us  [on_device(): call(block_kernel, [((2, CHUNKS, PART, 256), BF16), ((2, CHUNKS, PART, LA...]
where the time goes in v5:
time: 108 us
  Pallas kernels  107 us (99%)
    pallas_call x1, Pallas kernels, on_device(): call(block_kernel, [((2, CHUNKS, PART, 256), BF16), ((2, CHUNKS, PART, LA...  97.8 us
    pallas_call x1, Pallas kernels, on_device(): call(finish_kernel, [(lines, BF16), (lines, BF16), ((1, width), F32), ((1...  9.09 us

profile of v5, /device:TPU:1, one launch (start us, length us, event | category | flops | bytes accessed | tf_op | source)
XLA Modules:
  0.0 107.7 jit_solution(9499980529996488360)
XLA Ops:
  0.6 97.8 %block.1 = (bf16[2,4,1024,256]{3,2,1,0:T(8,128)(2,1)}, bf16[2,4,1024,128]{3,2,1,0:T(8,128)(2,1)}, f32[8,128]{1,0:T(8,128)}, bf16[288,512]{1,0:T(8,128)(2,1)}, bf...) custom-call(s32[4]{0:T(128)} %rows.3, s32[4]{0:T(128)} %cols.3, ...), custom_call_target="tpu_custom_call" | custom-call | tf_op jit(solution)/shard_map/block/pallas_call | solution.py:649
  98.4 9.1 %finish.1 = (bf16[72,4,512]{2,1,0:T(4,128)(2,1)}, bf16[72,4,512]{2,1,0:T(4,128)(2,1)}, f32[1,512]{1,0:T(1,128)}, f32[1,512]{1,0:T(1,128)}, f32[512,1536]{1,0:T(8...) custom-call(s32[4]{0:T(128)} %rows.3, s32[4]{0:T(128)} %cols.3, ...), custom_call_target="tpu_custom_call" | custom-call | tf_op jit(solution)/shard_map/finish/pallas_call | solution.py:693

commit v6 on v5

--- a/solution.py
+++ b/solution.py
@@ -22,17 +22,17 @@
 F32 = jnp.float32
 BF16 = jnp.bfloat16
 CHUNKS = 4
-FIRST_AXIS = (1, 2, 1, 0, 2, 1, 2, 2)
+ORDER = ((0, 1, 2), (1, 2, 0), (2, 0, 1), (2, 1, 0), (1, 0, 2), (1, 2, 0), (0, 1, 2), (2, 1, 0))
 GAINS, OUT, TOK = 8, 9, 10
 PUMP_MLP = ((0,), (1,), (2, 0), (3, 1, 2))
-PUMP_OUT, PUMP_MIX = (4, 3), ()
-PUMP_PAIRS = ((4,), (5,), (), (6, 7, 5, 0, 9, 6, 7, 1))
-PUMP_FRAME = ()
-PUMP_TAIL = (4, 8, 2, 3, 0, 5, 6, 1, 7, 10, 8, 3, 2, 4, 0, 6, 5, 1, 8, 7, 2, 4, 3, 6, 5, 7, 0, 8, 1, 0, 1, 4, 3, 2, 4, 6, 3, 5, 2, 6, 7, 5, 7)
+PUMP_OUT, PUMP_MIX = (4,), ()
+PUMP_PAIRS = ((3, 4), (5,), (), (6, 7, 5))
+PUMP_FRAME = (0, 6, 7, 1, 2)
+PUMP_TAIL = (8, 4, 9, 5, 3, 0, 6, 2, 7, 1, 5, 3, 6, 0, 2, 7, 8, 10, 4, 6, 0, 8, 1, 5, 3, 4, 8, 2, 7, 6, 1, 5, 3, 7, 0, 4, 0, 2, 6, 1, 2, 6, 1, 5, 3, 5, 4, 3, 7, 4, 7)
 PART = 1024
 QUARTER = 256
-SHARE = 16
-ROUNDS = 6
+SHARE = 64
+ROUNDS = 7
 VMEM_BYTES = 60 * 1024 * 1024
 DIMS_ZERO = (((0,), (0,)), ((), ()))
 DIMS_LAST = (((1,), (1,)), ((), ()))
@@ -83,17 +83,14 @@
     def away(offset):
         return device(*[p + o for p, o in zip(spot, offset)])
 
-    offsets = [(i, j, k) for i in range(SIDE) for j in range(SIDE) for k in range(SIDE)]
     peers = [[away([j * (a == b) for b in range(3)]) for j in range(1, SIDE)] for a in range(3)]
-    planes = [[(o, away(o)) for o in offsets if o[a] == 0 and any(o)] for a in range(3)]
-    known = [away(o) for o in offsets if 0 in o and any(o)]
     grid = {
         "below": (lax.rem(lat + 1, lats), lon),
         "above": (lax.rem(lat + lats - 1, lats), lon),
         "right": (lat, lax.rem(lon + 1, lons)),
         "left": (lat, lax.rem(lon + lons - 1, lons)),
     }
-    return grid, core, (y_hi * 2 + 1 - core, lon), peers, planes, known, spot
+    return grid, core, (y_hi * 2 + 1 - core, lon), peers, spot
 
 
 def remote(src, dst, send, recv, device):
@@ -159,19 +156,19 @@
     tok_above, cot_left, tok_rows, tok_left, cot_cols, cot_above, ids, ids_x,
     cotf, tokf, labf, norm_a, h_a, qkv, probs, mixed, resid, norm_m, h_m, dh, dqkv,
     out_f, out_right, tok_f, tok_right, out_t, out_tx, tok_t, tok_tx, gains_acc, gains_in,
-    part_a, core_a, mine_a, r1_a, m1_a, r2_a, total_a,
-    part_b, core_b, mine_b, r1_b, m1_b, r2_b, total_b,
+    part_a, core_a, mine_a, r1_a, m1_a, r2_a, m2_a, r3_a, total_a,
+    part_b, core_b, mine_b, r1_b, m1_b, r2_b, m2_b, r3_b, total_b,
     load_sem, halo_send, halo_recv, sum_send, sum_recv, gain_send, gain_recv, store_sem,
 ):
     width = gain_a.shape[1]
-    grid, core, core_peer, peers, planes, known, position = places()
+    grid, core, core_peer, peers, position = places()
     loads = [
         pltpu.make_async_copy(src, dst, load_sem.at[k])
         for k, (src, dst) in enumerate(
             ((w_qkv_hbm, w_qkv), (w_out_hbm, w_out), (w_up_hbm, w_up), (w_down_hbm, w_down))
         )
     ]
-    greeted = [core_peer] + known + list(grid.values())
+    greeted = [core_peer] + [p for axis in peers for p in axis] + list(grid.values())
     barrier = pltpu.get_barrier_semaphore()
     for device in greeted:
         pl.semaphore_signal(barrier, inc=1, device_id=device, device_id_type=MESH)
@@ -311,8 +308,8 @@
     arrived(lat_cot)
     cotf[...] = apply_roll(second_pair, cot_cols[...], cot_above[...])
 
-    set_a = (part_a, core_a, mine_a, r1_a, m1_a, r2_a, total_a, total_a_hbm)
-    set_b = (part_b, core_b, mine_b, r1_b, m1_b, r2_b, total_b, total_b_hbm)
+    set_a = (part_a, core_a, mine_a, r1_a, m1_a, r2_a, m2_a, r3_a, total_a, total_a_hbm)
+    set_b = (part_b, core_b, mine_b, r1_b, m1_b, r2_b, m2_b, r3_b, total_b, total_b_hbm)
     sent = []
 
     def block(offset, count):
@@ -324,15 +321,9 @@
         stores.append(copy)
 
     def chain(refs, i, k):
-        partial, core_in, mine, r1, m1, r2, total, total_hbm = refs
-        axis = FIRST_AXIS[k]
-        plane = planes[axis]
-        at = position[axis]
-        rest = [a for a in range(3) if a != axis]
-
-        def share(offset):
-            first, second = [lax.rem(position[a] + offset[a], SIDE) for a in rest]
-            return (first * SIDE + second) * SHARE
+        partial, core_in, mine, r1, m1, r2, m2, r3, total, total_hbm = refs
+        first, second, third = ORDER[k]
+        at, then = position[first], position[second]
 
         def send(n, src, dst, device):
             remote(src, dst, sum_send.at[k, n], sum_recv.at[k, n], device).start()
@@ -348,34 +339,42 @@
         mine[i] = (partial[core, i].astype(F32) + core_in[i].astype(F32)).astype(BF16)
         for j in range(1, SIDE):
             quarter = block(lax.rem(at + j, SIDE) * QUARTER, QUARTER)
-            send(1, mine.at[i, quarter], r1.at[i, j - 1], peers[axis][j - 1])
+            send(1, mine.at[i, quarter], r1.at[i, j - 1], peers[first][j - 1])
         yield
         arrive(1, r1.at[i])
         summed = mine[i, block(at * QUARTER, QUARTER), :].astype(F32)
         for j in range(SIDE - 1):
             summed = summed + r1[i, j].astype(F32)
         m1[i] = summed.astype(BF16)
-        for n, (offset, device) in enumerate(plane):
-            send(2, m1.at[i, block(share(offset), SHARE)], r2.at[i, n], device)
+        for j in range(1, SIDE):
+            share = block(lax.rem(then + j, SIDE) * SHARE, SHARE)
+            send(2, m1.at[i, share], r2.at[i, j - 1], peers[second][j - 1])
         yield
         arrive(2, r2.at[i])
-        own = share((0, 0, 0))
-        summed = m1[i, block(own, SHARE), :].astype(F32) + jnp.sum(r2[i].astype(F32), axis=0)
-        place = (core, i, block(at * QUARTER + own, SHARE))
-        total[place] = summed.astype(BF16)
-        for offset, device in plane:
-            send(3, total.at[place], total.at[place], device)
-        yield
-        arrive(3, r2.at[i])
+        summed = m1[i, block(then * SHARE, SHARE), :].astype(F32)
+        for j in range(SIDE - 1):
+            summed = summed + r2[i, j].astype(F32)
+        m2[i] = summed.astype(BF16)
+        for j in range(SIDE - 1):
+            send(3, m2.at[i], r3.at[i, j], peers[third][j])
+        yield
+        arrive(3, r3.at[i])
+        near, far = r3[i, 0].astype(F32) + r3[i, 2].astype(F32), m2[i].astype(F32) + r3[i, 1].astype(F32)
+        place = (core, i, block(at * QUARTER + then * SHARE, SHARE))
+        total[place] = (near + far).astype(BF16)
+        for device in peers[second]:
+            send(4, total.at[place], total.at[place], device)
+        yield
+        arrive(4, r2.at[i])
         place = (core, i, block(at * QUARTER, QUARTER))
-        for device in peers[axis]:
-            send(4, total.at[place], total.at[place], device)
-        yield
-        arrive(4, r1.at[i])
-        send(5, total.at[core, i], total.at[core, i], core_peer)
+        for device in peers[first]:
+            send(5, total.at[place], total.at[place], device)
+        yield
+        arrive(5, r1.at[i])
+        send(6, total.at[core, i], total.at[core, i], core_peer)
         store(total.at[core, i], total_hbm.at[core, i])
         yield
-        arrive(5, core_in.at[i])
+        arrive(6, core_in.at[i])
         store(total.at[1 - core, i], total_hbm.at[1 - core, i])
 
     def gain_chain():
@@ -528,19 +527,20 @@
 ):
     width = gain_a.shape[1]
     loads, moves = {}, []
-    for i in range(CHUNKS):
+
+    def load_group(i):
         for kind, (src, dst) in enumerate(((total_a_hbm, total_a), (total_b_hbm, total_b))):
             for half in range(2):
                 load = pltpu.make_async_copy(src.at[half, i], dst.at[half, i], in_sems.at[kind, half, i])
                 load.start()
                 loads[kind, half, i] = load
+
+    load_group(0)
+    load_group(1)
     tile_loads = [
         pltpu.make_async_copy(src, tiles.at[n], tile_sems.at[n])
         for n, src in enumerate((out_t_hbm, out_tx_hbm, tok_t_hbm, tok_tx_hbm))
     ]
-    for load in tile_loads:
-        load.start()
-
     def move(src, dst):
         copy = pltpu.make_async_copy(src, dst, out_sems.at[len(moves)])
         copy.start()
@@ -548,9 +548,14 @@
 
     homes = {(0, 1): (0, 0), (1, 1): (1, 0), (0, 2): (2, 0), (1, 2): (0, 1), (0, 3): (1, 1), (1, 3): (2, 1)}
     for i in range(CHUNKS):
+        if i == 2:
+            for load in tile_loads:
+                load.start()
         here = slice(i * 512, (i + 1) * 512)
         for half in range(2):
             loads[0, half, i].wait()
+            if half == 0 and i + 2 < CHUNKS:
+                load_group(i + 2)
             for b in range(2):
                 value = total_a[half, i, b * 512 : (b + 1) * 512, :].astype(F32)
                 if half == 0:
@@ -617,7 +622,9 @@
         (CHUNKS, PART, lanes),
         (CHUNKS, SIDE - 1, QUARTER, lanes),
         (CHUNKS, QUARTER, lanes),
-        (CHUNKS, SIDE * SIDE - 1, SHARE, lanes),
+        (CHUNKS, SIDE - 1, SHARE, lanes),
+        (CHUNKS, SHARE, lanes),
+        (CHUNKS, SIDE - 1, SHARE, lanes),
         (2, CHUNKS, PART, lanes),
     ]
     return [pltpu.VMEM(shape, BF16) for shape in shapes]

time: 108 us -> 103 us (0.954)
  Pallas kernels: 107 us -> 102 us
    pallas_call x1, Pallas kernels: 97.8 us -> 93 us  [on_device(): call(block_kernel, [((2, CHUNKS, PART, 256), BF16), ((2, CHUNKS, PART, LA...]
where the time goes in v6:
time: 103 us
  Pallas kernels  102 us (99%)
    pallas_call x1, Pallas kernels, on_device(): call(block_kernel, [((2, CHUNKS, PART, 256), BF16), ((2, CHUNKS, PART, LA...  93 us
    pallas_call x1, Pallas kernels, on_device(): call(finish_kernel, [(lines, BF16), (lines, BF16), ((1, width), F32), ((1...  9.15 us

profile of v6, /device:TPU:1, one launch (start us, length us, event | category | flops | bytes accessed | tf_op | source)
XLA Modules:
  0.0 102.9 jit_solution(14163967645104989076)
XLA Ops:
  0.6 93.0 %block.1 = (bf16[2,4,1024,256]{3,2,1,0:T(8,128)(2,1)}, bf16[2,4,1024,128]{3,2,1,0:T(8,128)(2,1)}, f32[8,128]{1,0:T(8,128)}, bf16[288,512]{1,0:T(8,128)(2,1)}, bf...) custom-call(s32[4]{0:T(128)} %rows.3, s32[4]{0:T(128)} %cols.3, ...), custom_call_target="tpu_custom_call" | custom-call | tf_op jit(solution)/shard_map/block/pallas_call | solution.py:656
  93.6 9.1 %finish.1 = (bf16[72,4,512]{2,1,0:T(4,128)(2,1)}, bf16[72,4,512]{2,1,0:T(4,128)(2,1)}, f32[1,512]{1,0:T(1,128)}, f32[1,512]{1,0:T(1,128)}, f32[512,1536]{1,0:T(8...) custom-call(s32[4]{0:T(128)} %rows.3, s32[4]{0:T(128)} %cols.3, ...), custom_call_target="tpu_custom_call" | custom-call | tf_op jit(solution)/shard_map/finish/pallas_call | solution.py:700

commit v7 on v6

--- a/solution.py
+++ b/solution.py
@@ -26,8 +26,8 @@
 GAINS, OUT, TOK = 8, 9, 10
 PUMP_MLP = ((0,), (1,), (2, 0), (3, 1, 2))
 PUMP_OUT, PUMP_MIX = (4,), ()
-PUMP_PAIRS = ((3, 4), (5,), (), (6, 7, 5))
-PUMP_FRAME = (0, 6, 7, 1, 2)
+PUMP_PAIRS = ((3, 4), (5,), (), (6, 7))
+PUMP_FRAME = (5, 0, 6, 7, 1, 2)
 PUMP_TAIL = (8, 4, 9, 5, 3, 0, 6, 2, 7, 1, 5, 3, 6, 0, 2, 7, 8, 10, 4, 6, 0, 8, 1, 5, 3, 4, 8, 2, 7, 6, 1, 5, 3, 7, 0, 4, 0, 2, 6, 1, 2, 6, 1, 5, 3, 5, 4, 3, 7, 4, 7)
 PART = 1024
 QUARTER = 256

time: 103 us -> 103 us (level)
  no operation moved by 1% of the time
where the time goes in v7:
time: 103 us
  Pallas kernels  102 us (99%)
    pallas_call x1, Pallas kernels, on_device(): call(block_kernel, [((2, CHUNKS, PART, 256), BF16), ((2, CHUNKS, PART, LA...  93 us
    pallas_call x1, Pallas kernels, on_device(): call(finish_kernel, [(lines, BF16), (lines, BF16), ((1, width), F32), ((1...  9.14 us

profile of v7, /device:TPU:1, one launch (start us, length us, event | category | flops | bytes accessed | tf_op | source)
XLA Modules:
  0.0 103.0 jit_solution(4588649753308693491)
XLA Ops:
  0.6 93.0 %block.1 = (bf16[2,4,1024,256]{3,2,1,0:T(8,128)(2,1)}, bf16[2,4,1024,128]{3,2,1,0:T(8,128)(2,1)}, f32[8,128]{1,0:T(8,128)}, bf16[288,512]{1,0:T(8,128)(2,1)}, bf...) custom-call(s32[4]{0:T(128)} %rows.3, s32[4]{0:T(128)} %cols.3, ...), custom_call_target="tpu_custom_call" | custom-call | tf_op jit(solution)/shard_map/block/pallas_call | solution.py:656
  93.7 9.1 %finish.1 = (bf16[72,4,512]{2,1,0:T(4,128)(2,1)}, bf16[72,4,512]{2,1,0:T(4,128)(2,1)}, f32[1,512]{1,0:T(1,128)}, f32[1,512]{1,0:T(1,128)}, f32[512,1536]{1,0:T(8...) custom-call(s32[4]{0:T(128)} %rows.3, s32[4]{0:T(128)} %cols.3, ...), custom_call_target="tpu_custom_call" | custom-call | tf_op jit(solution)/shard_map/finish/pallas_call | solution.py:700
